TPU v7x, 128 devices: a whole 4x4x4 slice. The times are simulated.
128 devices in a mesh: dp: 8 (over x, y_lo), owner: 16 (over y_hi, z, core).
Axes of the slice: x: 4, y: 4 (y_hi: 2, y_lo: 2; y = y_hi * 2 + y_lo), z: 4, core: 2. Of those that a mesh axis runs over, the one named last changes fastest.
Arguments:
- grad_partials: bfloat16 [8, 128, 512, 512], P('dp', 'owner'), may hold values from -2.5 to 2.5
- owner_slot: int32 [16, 8], replicated, may hold values from 0 to 7, each once within a row
- refresh_blocks: int32 [32], replicated, may hold values from 0 to 127, as said below
- left_stat: float32 [16, 8, 512, 512], P('owner', 'dp'), as said below
- right_stat: float32 [16, 8, 512, 512], P('owner', 'dp'), as said below
- left_root: bfloat16 [16, 8, 512, 512], P('owner', 'dp'), as said below
- right_root: bfloat16 [16, 8, 512, 512], P('owner', 'dp'), as said below
Outputs:
- update: bfloat16 [16, 8, 512, 512], P(None, 'dp')
- left_stat_new: float32 [16, 8, 512, 512], P('owner', 'dp')
- right_stat_new: float32 [16, 8, 512, 512], P('owner', 'dp')
- left_root_new: bfloat16 [16, 8, 512, 512], P('owner', 'dp')
- right_root_new: bfloat16 [16, 8, 512, 512], P('owner', 'dp')
Inputs may be any that keep to these rules, and one draw needn't show every extreme that they name: `owner_slot`: each row is an ordering of the 8 slots of one owner group. `refresh_blocks`: 32 distinct block numbers, always including block 0 and block 127. `left_stat`: each block is symmetric positive definite. `right_stat`: each block is symmetric positive definite. `left_root`: each block is symmetric. `right_root`: each block is symmetric.
All inputs are finite; a program needn't handle non-finite values.
Results may differ from a plain program's by a relative error of at most 0.02.
Values may be sent and summed in bfloat16 or wider, within the bound.
A program may use at most 128 MiB of HBM per device.

v0:
```python
import jax
import jax.numpy as jnp
from jax import lax
from jax.experimental import pallas as pl
from jax.experimental.pallas import tpu as pltpu
from jax.sharding import PartitionSpec as P

MESH = pl.DeviceIdType.MESH
f32 = jnp.float32
bf16 = jnp.bfloat16

N = 512
XS, ZS, SLOTS, REFRESH = 4, 4, 8, 32
decay_rate = 0.8
graft_eps = 1e-06

RA, RAH = 288, 144
RB, RBH = N - RA, (N - RA) // 2
A_LO, A_HI, A_ALL = pl.ds(0, RAH), pl.ds(RAH, RAH), pl.ds(0, RA)
B_LO, B_HI, B_ALL = pl.ds(RA, RBH), pl.ds(RA + RBH, RBH), pl.ds(RA, RB)
LO_A, HI_A = pl.ds(0, RAH), pl.ds(RAH, RAH)
LO_B, HI_B = pl.ds(0, RBH), pl.ds(RBH, RBH)


def position():
    dp, ow = lax.axis_index("dp"), lax.axis_index("owner")
    return dp // 2, dp % 2, ow // 8, (ow // 2) % 4, ow % 2


def greet(targets):
    barrier = pltpu.get_barrier_semaphore()
    for target in targets:
        pl.semaphore_signal(barrier, inc=1, device_id=target, device_id_type=MESH)
    pl.semaphore_wait(barrier, len(targets))


class Copies:
    def __init__(self, send_sem, recv_sem):
        self.send_sem, self.recv_sem, self.started = send_sem, recv_sem, {}

    def start(self, name, src, dst, target):
        at = len(self.started)
        copy = pltpu.make_async_remote_copy(
            src_ref=src, dst_ref=dst, send_sem=self.send_sem.at[at], recv_sem=self.recv_sem.at[at],
            device_id=target, device_id_type=MESH)
        copy.start()
        self.started[name] = copy

    def arrived(self, *names):
        for name in names:
            self.started[name].wait_recv()

    def finish(self):
        for copy in self.started.values():
            copy.wait_send()


def reduce_kernel(owner_slot, partials, g_ref, st, ra1, ra2, ra3, rb1, sb, rb2, rb3, acc_a, acc_b, sum_a, send_sem, recv_sem):
    x, yl, yh, z, c = position()
    dp, ow = lax.axis_index("dp"), lax.axis_index("owner")
    xp = (((x + 1) % XS) * 2 + yl, ow)
    xm = (((x + XS - 1) % XS) * 2 + yl, ow)
    yo = (x * 2 + 1 - yl, ow)
    greet((xp, xm, yo))
    go = Copies(send_sem, recv_sem)

    def block_of(dx, dy):
        slot = ((x + dx) % XS) * 2 + (yl + dy) % 2
        found = jnp.int32(0)
        for r in range(SLOTS):
            found = jnp.where(owner_slot[ow, r] == slot, jnp.int32(r), found)
        return found

    where = {(dx, dy): block_of(dx, dy) for dx in range(XS) for dy in range(2)}

    def stage(dx, dy, rows):
        st[dx * 2 + dy, rows, :] = partials[where[dx, dy], rows, :]

    def own(dx, dy, rows):
        return st.at[dx * 2 + dy, rows]

    def first_a(dy):
        stage(2, dy, A_ALL)
        go.start(("a1p", dy), own(2, dy, A_LO), ra1.at[0, dy], xp)
        go.start(("a1m", dy), own(2, dy, A_HI), ra1.at[1, dy], xm)

    def own_a(dy):
        stage(1, dy, A_ALL)
        go.start(("a2p", dy), own(1, dy, A_HI), ra2.at[0, dy, HI_A], xp)
        stage(3, dy, A_ALL)
        go.start(("a2m", dy), own(3, dy, A_LO), ra2.at[1, dy, LO_A], xm)

    def sum_of_a(dy):
        go.arrived(("a1p", dy), ("a1m", dy))
        acc_a[0, dy] = (st[2 + dy, A_LO, :].astype(f32) + ra1[0, dy].astype(f32)).astype(bf16)
        go.start(("a3p", dy), acc_a.at[0, dy], ra2.at[0, dy, LO_A], xp)
        acc_a[1, dy] = (st[6 + dy, A_HI, :].astype(f32) + ra1[1, dy].astype(f32)).astype(bf16)
        go.start(("a3m", dy), acc_a.at[1, dy], ra2.at[1, dy, HI_A], xm)

    def first_b(dx):
        stage(dx, 1, B_ALL)
        go.start(("b1", dx), own(dx, 1, B_ALL), rb1.at[dx], yo)

    def sum_of_b(dx):
        stage(dx, 0, B_ALL)
        go.arrived(("b1", dx))
        sb[dx] = (st[dx * 2, B_ALL, :].astype(f32) + rb1[dx].astype(f32)).astype(bf16)

    first_a(1)
    first_b(2)
    first_a(0)
    own_a(1)
    first_b(1)
    stage(0, 0, A_ALL)
    stage(0, 1, A_ALL)
    sum_of_a(1)
    sum_of_b(2)
    first_b(3)
    own_a(0)
    sum_of_a(0)
    go.start("b2p", sb.at[2, LO_B], rb2.at[0], xp)
    go.start("b2m", sb.at[2, HI_B], rb2.at[1], xm)
    sum_of_b(1)
    first_b(0)
    go.start("b3p", sb.at[1, HI_B], rb3.at[0, HI_B], xp)
    go.arrived(("a2p", 1), ("a2m", 1), ("a3p", 1), ("a3m", 1))
    sum_a[...] = (st[1, A_ALL, :].astype(f32) + ra2[0, 1].astype(f32) + ra2[1, 1].astype(f32)).astype(bf16)
    go.start("a4", sum_a, ra3, yo)
    sum_of_b(3)
    go.start("b3m", sb.at[3, LO_B], rb3.at[1, LO_B], xm)
    go.arrived("b2p", "b2m")
    acc_b[0] = (sb[1, LO_B, :].astype(f32) + rb2[0].astype(f32)).astype(bf16)
    go.start("b4p", acc_b.at[0], rb3.at[0, LO_B], xp)
    acc_b[1] = (sb[3, HI_B, :].astype(f32) + rb2[1].astype(f32)).astype(bf16)
    go.start("b4m", acc_b.at[1], rb3.at[1, HI_B], xm)
    go.arrived(("a2p", 0), ("a2m", 0), ("a3p", 0), ("a3m", 0))
    stage(0, 0, B_ALL)
    go.arrived(("b1", 0))
    go.arrived("a4")
    g_ref[A_ALL, :] = (st[0, A_ALL, :].astype(f32) + ra2[0, 0].astype(f32) + ra2[1, 0].astype(f32)
                       + ra3[...].astype(f32)).astype(bf16)
    go.arrived("b3p", "b3m", "b4p", "b4m")
    g_ref[B_ALL, :] = (st[0, B_ALL, :].astype(f32) + rb1[0].astype(f32) + rb3[0].astype(f32)
                       + rb3[1].astype(f32)).astype(bf16)
    go.finish()


def reduce_scatter(owner_slot, partials):
    vm = lambda *shape: pltpu.VMEM(shape + (N,), bf16)
    return pl.pallas_call(
        reduce_kernel,
        out_shape=jax.ShapeDtypeStruct((N, N), bf16),
        in_specs=[pl.BlockSpec(memory_space=pltpu.SMEM), pl.BlockSpec(memory_space=pltpu.VMEM)],
        out_specs=pl.BlockSpec(memory_space=pltpu.VMEM),
        scratch_shapes=[
            vm(SLOTS, N), vm(2, 2, RAH), vm(2, 2, RA), vm(RA), vm(XS, RB), vm(XS, RB), vm(2, RBH), vm(2, RB),
            vm(2, 2, RAH), vm(2, RBH), vm(RA),
            pltpu.SemaphoreType.DMA((23,)), pltpu.SemaphoreType.DMA((23,)),
        ],
        compiler_params=pltpu.CompilerParams(collective_id=0, has_side_effects=True, vmem_limit_bytes=40 * 2**20),
        name="reduce_scatter",
    )(owner_slot, partials)


def dot(a, b):
    return jnp.dot(a, b, preferred_element_type=f32)


def split(a):
    high = a.astype(bf16)
    return high, (a - high.astype(f32)).astype(bf16)


def total(a):
    return jnp.sum(jnp.sum(a, axis=0, keepdims=True), axis=1, keepdims=True)


def root(stat):
    rows = lax.broadcasted_iota(jnp.int32, (N, N), 0)
    cols = lax.broadcasted_iota(jnp.int32, (N, N), 1)
    eye = jnp.where(rows == cols, 1.0, 0.0).astype(f32)
    scale = total(stat * eye) * (2.0 / N)
    d = (eye - stat * (1.0 / scale)) * 0.25
    h = eye + d
    dh, dl = split(d)
    d2 = dot(dh, dh) + (dot(dh, dl) + dot(dl, dh))
    d2h, d2l = split(d2)
    d3 = dot(dh, d2h) + (dot(dh, d2l) + dot(dl, d2h))
    uh, ul = split(3.75 * d2 + d3)
    d = 2.5 * d2 + 5.0 * d3 + (dot(d2h, uh) + (dot(d2h, ul) + dot(d2l, uh)))
    for sweep in range(3):
        low = d.astype(bf16)
        h = h + dot(h.astype(bf16), low)
        if sweep == 2:
            break
        d2 = dot(low, low)
        d2h = d2.astype(bf16)
        d3 = dot(low, d2h)
        d = 2.5 * d2 + 5.0 * d3 + dot(d2h, (3.75 * d2 + d3).astype(bf16))
    return h * lax.rsqrt(jnp.sqrt(scale))


def local_kernel(owner_slot, refresh, g_ref, left_stat, right_stat, left_root, right_root,
                 update, left_new, right_new, left_out, right_out):
    dp, ow = lax.axis_index("dp"), lax.axis_index("owner")
    block = ow * SLOTS
    for r in range(SLOTS):
        block = block + jnp.where(owner_slot[ow, r] == dp, jnp.int32(r), jnp.int32(0))
    hits = jnp.int32(0)
    for i in range(REFRESH):
        hits = hits + jnp.where(refresh[i] == block, jnp.int32(1), jnp.int32(0))
    g = g_ref[...]
    gt = g.T
    weight = (1.0 - decay_rate) / N
    left_new[...] = decay_rate * left_stat[...] + weight * dot(g, gt)
    right_new[...] = decay_rate * right_stat[...] + weight * dot(gt, g)

    @pl.when(hits > 0)
    def _():
        left_out[...] = root(left_new[...]).astype(bf16)
        right_out[...] = root(right_new[...]).astype(bf16)

    @pl.when(hits == 0)
    def _():
        left_out[...] = left_root[...]
        right_out[...] = right_root[...]

    raw = dot(dot(left_out[...], g).astype(bf16), right_out[...])
    gf = g.astype(f32)
    graft = jnp.sqrt(total(gf * gf) * (1.0 / (N * N))) / jnp.sqrt(total(raw * raw) * (1.0 / (N * N)) + graft_eps)
    update[...] = (raw * graft).astype(bf16)


def local_step(owner_slot, refresh, g, left_stat, right_stat, left_root, right_root):
    vmem, smem = pl.BlockSpec(memory_space=pltpu.VMEM), pl.BlockSpec(memory_space=pltpu.SMEM)
    like = lambda dtype: jax.ShapeDtypeStruct((N, N), dtype)
    return pl.pallas_call(
        local_kernel,
        out_shape=(like(bf16), like(f32), like(f32), like(bf16), like(bf16)),
        in_specs=[smem] * 2 + [vmem] * 5,
        out_specs=[vmem] * 5,
        compiler_params=pltpu.CompilerParams(vmem_limit_bytes=40 * 2**20),
        name="local_step",
    )(owner_slot, refresh, g, left_stat, right_stat, left_root, right_root)


RY, RYH = 288, 144
RZ, RZH = N - RY, (N - RY) // 2
Y_ALL, Y_LO, Y_HI = pl.ds(0, RY), pl.ds(0, RYH), pl.ds(RYH, RYH)
Z_ALL, Z_LO, Z_HI = pl.ds(RY, RZ), pl.ds(RY, RZH), pl.ds(RY + RZH, RZH)


def gather_kernel(update, out, send_sem, recv_sem):
    x, yl, yh, z, c = position()
    dp, ow = lax.axis_index("dp"), lax.axis_index("owner")

    def owner(dz, dy, dc=0):
        return (((yh + dy) % 2) * ZS + (z + dz) % ZS) * 2 + (c + dc) % 2

    zp, zm = (dp, owner(1, 0)), (dp, owner(3, 0))
    yo, co = (dp, owner(0, 1)), (dp, owner(0, 0, 1))
    greet((zp, zm, yo, co))
    go = Copies(send_sem, recv_sem)

    def pass_on(name, dz, dy, rows, target):
        piece = out.at[owner(dz, dy), rows]
        go.start(name, piece, piece, target)

    def share(dz, dy, rows, tag):
        pass_on(("core", dz, dy, tag), dz, dy, rows, co)

    def mine(name, rows, target):
        go.start(name, update.at[rows], out.at[owner(0, 0), rows], target)

    mine("yY", Y_ALL, yo)
    mine("zZ+", Z_ALL, zp)
    mine("zZ-", Z_ALL, zm)
    mine("zY+", Y_ALL, zp)
    mine("zY-", Y_ALL, zm)
    mine("yZ", Z_ALL, yo)
    mine("core", pl.ds(0, N), co)
    out[owner(0, 0)] = update[...]

    go.arrived("zZ+")
    pass_on("zZ2+", 3, 0, Z_LO, zp)
    pass_on("yZ-", 3, 0, Z_ALL, yo)
    share(3, 0, Z_ALL, "Z")
    go.arrived("zZ-")
    pass_on("zZ2-", 1, 0, Z_HI, zm)
    pass_on("yZ+", 1, 0, Z_ALL, yo)
    share(1, 0, Z_ALL, "Z")
    go.arrived("yY")
    pass_on("pY+", 0, 1, Y_ALL, zp)
    pass_on("pY-", 0, 1, Y_ALL, zm)
    share(0, 1, Y_ALL, "Y")
    go.arrived("zY+")
    pass_on("zY2+", 3, 0, Y_LO, zp)
    share(3, 0, Y_ALL, "Y")
    go.arrived("zY-")
    pass_on("zY2-", 1, 0, Y_HI, zm)
    share(1, 0, Y_ALL, "Y")
    go.arrived("yZ")
    share(0, 1, Z_ALL, "Z")
    go.arrived("zZ2+", "zZ2-")
    pass_on("yZ2", 2, 0, Z_ALL, yo)
    share(2, 0, Z_ALL, "Z")
    go.arrived("yZ-")
    share(3, 1, Z_ALL, "Z")
    go.arrived("pY+")
    pass_on("pY2+", 3, 1, Y_LO, zp)
    share(3, 1, Y_ALL, "Y")
    go.arrived("pY-")
    pass_on("pY2-", 1, 1, Y_HI, zm)
    share(1, 1, Y_ALL, "Y")
    go.arrived("yZ+")
    share(1, 1, Z_ALL, "Z")
    go.arrived("zY2+", "zY2-")
    share(2, 0, Y_ALL, "Y")
    go.arrived("yZ2")
    share(2, 1, Z_ALL, "Z")
    go.arrived("pY2+", "pY2-")
    share(2, 1, Y_ALL, "Y")
    go.arrived("core", *[name for name in go.started if name[0] == "core" and len(name) == 4 and name != "core"])
    go.finish()


def all_gather(update):
    copies = 12 + 6 + 15
    return pl.pallas_call(
        gather_kernel,
        out_shape=jax.ShapeDtypeStruct((16, N, N), bf16),
        in_specs=[pl.BlockSpec(memory_space=pltpu.VMEM)],
        out_specs=pl.BlockSpec(memory_space=pltpu.VMEM),
        scratch_shapes=[pltpu.SemaphoreType.DMA((copies,)), pltpu.SemaphoreType.DMA((copies,))],
        compiler_params=pltpu.CompilerParams(collective_id=1, has_side_effects=True, vmem_limit_bytes=40 * 2**20),
        name="all_gather",
    )(update)


def body(grad_partials, owner_slot, refresh_blocks, left_stat, right_stat, left_root, right_root):
    g = reduce_scatter(owner_slot, grad_partials[0])
    update, left_new, right_new, left_out, right_out = local_step(
        owner_slot, refresh_blocks, g, left_stat[0, 0], right_stat[0, 0], left_root[0, 0], right_root[0, 0])
    gathered = all_gather(update)
    return (gathered[:, None], left_new[None, None], right_new[None, None], left_out[None, None], right_out[None, None])


def solution(mesh):
    slots = P("owner", "dp", None, None)
    return jax.shard_map(
        body,
        mesh=mesh,
        in_specs=(P("dp", "owner", None, None), P(), P(), slots, slots, slots, slots),
        out_specs=(P(None, "dp", None, None), slots, slots, slots, slots),
        check_vma=False,
    )
```

profile of v0, /device:TPU:1, one launch (start us, length us, event | category | flops | bytes accessed | tf_op | source)
XLA Modules:
  0.0 102.8 jit_solution(9604194708833448308)
XLA Ops:
  0.6 0.8 copy.13.owner_slot
  1.4 0.0 copy-start.1
  1.4 2.2 %copy-done.1 = bf16[1,8,512,512]{3,2,1,0:T(8,128)(2,1)S(1)} copy-done((bf16[1,8,512,512]{3,2,1,0:T(8,128)(2,1)S(1)}, bf16[1,8,512,512]{3,2,1,0:T(8,128)(2,1)}, u32[]{:S(2)}) %copy-start.1) | copy-done | bytes 4194328
  3.6 32.1 %reduce_scatter.1.g_ref = bf16[512,512]{1,0:T(8,128)(2,1)S(1)} custom-call(s32[16,8]{1,0:T(8,128)S(1)} %copy.13.owner_slot, bf16[8,512,512]{2,1,0:T(8,128)(2,1)S(1)} %bitcast.13), custom_call_target="tpu_custom_call" | custom-call | tf_op jit(solution)/shard_map/reduce_scatter/pallas_call | solution.py:150
  35.7 0.0 copy-start.2
  35.7 1.2 %copy-done.2 = f32[1,1,512,512]{3,2,1,0:T(8,128)S(1)} copy-done((f32[1,1,512,512]{3,2,1,0:T(8,128)S(1)}, f32[1,1,512,512]{3,2,1,0:T(8,128)}, u32[]{:S(2)}) %copy-start.2) | copy-done | bytes 1048600
  36.9 0.0 copy-start.3
  36.9 1.2 %copy-done.3 = f32[1,1,512,512]{3,2,1,0:T(8,128)S(1)} copy-done((f32[1,1,512,512]{3,2,1,0:T(8,128)S(1)}, f32[1,1,512,512]{3,2,1,0:T(8,128)}, u32[]{:S(2)}) %copy-start.3) | copy-done | bytes 1048600
  38.2 0.0 copy-start.4
  38.2 1.0 %copy-done.4 = bf16[1,1,512,512]{3,2,1,0:T(8,128)(2,1)S(1)} copy-done((bf16[1,1,512,512]{3,2,1,0:T(8,128)(2,1)S(1)}, bf16[1,1,512,512]{3,2,1,0:T(8,128)(2,1)}, u32[]{:S(2)}) %copy-start.4) | copy-done | bytes 524312
  39.2 0.0 copy-start.5
  39.2 1.0 %copy-done.5 = bf16[1,1,512,512]{3,2,1,0:T(8,128)(2,1)S(1)} copy-done((bf16[1,1,512,512]{3,2,1,0:T(8,128)(2,1)S(1)}, bf16[1,1,512,512]{3,2,1,0:T(8,128)(2,1)}, u32[]{:S(2)}) %copy-start.5) | copy-done | bytes 524312
  40.2 0.0 copy-start.6
  40.2 0.7 copy-done.6
  40.9 3.2 %local_step.1 = (bf16[512,512]{1,0:T(8,128)(2,1)S(1)}, f32[512,512]{1,0:T(8,128)}, f32[512,512]{1,0:T(8,128)}, bf16[512,512]{1,0:T(8,128)(2,1)}, bf16[512,512]{1,0:T(8,128)(2,1)}) custom-call(s32[16,8]{1,0:T(8,128)S(1)} %copy.13.owner_slot, s32[32]{0:T(128)S(1)} %copy-done.6, bf16[512,512]{1,0:T(8,128)(2,1)S(1)} %reduce_scatter.1.g_ref, ...), custom_call_target="tpu_custom_call" | custom-call | tf_op jit(solution)/shard_map/local_step/pallas_call | solution.py:237
  44.1 47.9 %all_gather.1 = bf16[16,512,512]{2,1,0:T(8,128)(2,1)S(1)} custom-call(bf16[512,512]{1,0:T(8,128)(2,1)S(1)} %get-tuple-element.10.update), custom_call_target="tpu_custom_call" | custom-call | tf_op jit(solution)/shard_map/all_gather/pallas_call | solution.py:329
  92.0 0.0 copy-start
  92.0 3.2 %copy-done = bf16[16,512,512]{2,1,0:T(8,128)(2,1)} copy-done((bf16[16,512,512]{2,1,0:T(8,128)(2,1)}, bf16[16,512,512]{2,1,0:T(8,128)(2,1)S(1)}, u32[]{:S(2)}) %copy-start) | copy-done | bytes 8388632
  95.3 7.5 %copy.16 = bf16[16,1,512,512]{3,2,1,0:T(8,128)(2,1)} copy(bf16[16,1,512,512]{3,2,1,0:T(8,128)(2,1)} %bitcast.12) | data formatting | bytes 16777216
Async XLA Ops:
  1.4 2.2 %copy-start.1 = (bf16[1,8,512,512]{3,2,1,0:T(8,128)(2,1)S(1)}, bf16[1,8,512,512]{3,2,1,0:T(8,128)(2,1)}, u32[]{:S(2)}) copy-start(bf16[1,8,512,512]{3,2,1,0:T(8,128)(2,1)} %param.7) | copy-start | bytes 12582916
  35.7 1.2 %copy-start.2 = (f32[1,1,512,512]{3,2,1,0:T(8,128)S(1)}, f32[1,1,512,512]{3,2,1,0:T(8,128)}, u32[]{:S(2)}) copy-start(f32[1,1,512,512]{3,2,1,0:T(8,128)} %param.10) | copy-start | bytes 3145732
  36.9 1.2 %copy-start.3 = (f32[1,1,512,512]{3,2,1,0:T(8,128)S(1)}, f32[1,1,512,512]{3,2,1,0:T(8,128)}, u32[]{:S(2)}) copy-start(f32[1,1,512,512]{3,2,1,0:T(8,128)} %param.11) | copy-start | bytes 3145732
  38.2 1.0 %copy-start.4 = (bf16[1,1,512,512]{3,2,1,0:T(8,128)(2,1)S(1)}, bf16[1,1,512,512]{3,2,1,0:T(8,128)(2,1)}, u32[]{:S(2)}) copy-start(bf16[1,1,512,512]{3,2,1,0:T(8,128)(2,1)} %param.12) | copy-start | bytes 1572868
  39.2 1.0 %copy-start.5 = (bf16[1,1,512,512]{3,2,1,0:T(8,128)(2,1)S(1)}, bf16[1,1,512,512]{3,2,1,0:T(8,128)(2,1)}, u32[]{:S(2)}) copy-start(bf16[1,1,512,512]{3,2,1,0:T(8,128)(2,1)} %param.13) | copy-start | bytes 1572868
  40.2 0.7 copy-start.6
  92.0 3.2 %copy-start = (bf16[16,512,512]{2,1,0:T(8,128)(2,1)}, bf16[16,512,512]{2,1,0:T(8,128)(2,1)S(1)}, u32[]{:S(2)}) copy-start(bf16[16,512,512]{2,1,0:T(8,128)(2,1)S(1)} %all_gather.1) | copy-start | bytes 25165828
where the time goes:
time: 103 us
  Pallas kernels  83.2 us (81%)
  local copies, waits for them, and re-layouts  18.9 us (18%)
    pallas_call x1, Pallas kernels, all_gather(): pl.pallas_call(gather_kernel, out_shape=jax.ShapeDtypeStruct((16, N, N),...  47.9 us
    pallas_call x1, Pallas kernels, reduce_scatter(): pl.pallas_call(reduce_kernel, out_shape=jax.ShapeDtypeStruct((N, N), bf16...  32.1 us
    unnamed x16, local copies, waits for them, and re-layouts  18.9 us
    pallas_call x1, Pallas kernels, local_step(): pl.pallas_call(local_kernel, out_shape=(like(bf16), like(f32), like(f32),...  3.24 us

commit v1 on v0

v1 whole, which is shorter than its diff:
```python
import jax
import jax.numpy as jnp
from jax import lax
from jax.experimental import pallas as pl
from jax.experimental.pallas import tpu as pltpu
from jax.sharding import PartitionSpec as P

MESH = pl.DeviceIdType.MESH
f32 = jnp.float32
bf16 = jnp.bfloat16

N = 512
XS, ZS, SLOTS, REFRESH = 4, 4, 8, 32
decay_rate = 0.8
graft_eps = 1e-06

RA, RAH = 288, 144
RB, RBH = N - RA, (N - RA) // 2
A_LO, A_HI, A_ALL = pl.ds(0, RAH), pl.ds(RAH, RAH), pl.ds(0, RA)
B_LO, B_HI, B_ALL = pl.ds(RA, RBH), pl.ds(RA + RBH, RBH), pl.ds(RA, RB)
LO_A, HI_A = pl.ds(0, RAH), pl.ds(RAH, RAH)
LO_B, HI_B = pl.ds(0, RBH), pl.ds(RBH, RBH)


def position():
    dp, ow = lax.axis_index("dp"), lax.axis_index("owner")
    return dp // 2, dp % 2, ow // 8, (ow // 2) % 4, ow % 2


def greet(targets):
    barrier = pltpu.get_barrier_semaphore()
    for target in targets:
        pl.semaphore_signal(barrier, inc=1, device_id=target, device_id_type=MESH)
    pl.semaphore_wait(barrier, len(targets))


class Copies:
    def __init__(self, send_sem, recv_sem):
        self.send_sem, self.recv_sem, self.started = send_sem, recv_sem, {}

    def start(self, name, src, dst, target):
        at = len(self.started)
        copy = pltpu.make_async_remote_copy(
            src_ref=src, dst_ref=dst, send_sem=self.send_sem.at[at], recv_sem=self.recv_sem.at[at],
            device_id=target, device_id_type=MESH)
        copy.start()
        self.started[name] = copy

    def arrived(self, *names):
        for name in names:
            self.started[name].wait_recv()

    def finish(self):
        for copy in self.started.values():
            copy.wait_send()


RY, RYH = 288, 144
RZ, RZH = N - RY, (N - RY) // 2
Y_ALL, Y_LO, Y_HI = pl.ds(0, RY), pl.ds(0, RYH), pl.ds(RYH, RYH)
Z_ALL, Z_LO, Z_HI = pl.ds(RY, RZ), pl.ds(RY, RZH), pl.ds(RY + RZH, RZH)


def dot(a, b):
    return jnp.dot(a, b, preferred_element_type=f32)


def split(a):
    high = a.astype(bf16)
    return high, (a - high.astype(f32)).astype(bf16)


def total(a):
    return jnp.sum(jnp.sum(a, axis=0, keepdims=True), axis=1, keepdims=True)


def root(stat):
    rows = lax.broadcasted_iota(jnp.int32, (N, N), 0)
    cols = lax.broadcasted_iota(jnp.int32, (N, N), 1)
    eye = jnp.where(rows == cols, 1.0, 0.0).astype(f32)
    scale = total(stat * eye) * (2.0 / N)
    d = (eye - stat * (1.0 / scale)) * 0.25
    h = eye + d
    dh, dl = split(d)
    d2 = dot(dh, dh) + (dot(dh, dl) + dot(dl, dh))
    d2h, d2l = split(d2)
    d3 = dot(dh, d2h) + (dot(dh, d2l) + dot(dl, d2h))
    uh, ul = split(3.75 * d2 + d3)
    d = 2.5 * d2 + 5.0 * d3 + (dot(d2h, uh) + (dot(d2h, ul) + dot(d2l, uh)))
    for sweep in range(3):
        low = d.astype(bf16)
        h = h + dot(h.astype(bf16), low)
        if sweep == 2:
            break
        d2 = dot(low, low)
        d2h = d2.astype(bf16)
        d3 = dot(low, d2h)
        d = 2.5 * d2 + 5.0 * d3 + dot(d2h, (3.75 * d2 + d3).astype(bf16))
    return h * lax.rsqrt(jnp.sqrt(scale))


def step_kernel(owner_slot, refresh, partials_hbm, left_stat_hbm, right_stat_hbm, left_root_hbm, right_root_hbm,
                out, left_new, right_new, left_out, right_out,
                partials, left_stat, right_stat, left_root, right_root, g, update,
                st, ra1, ra2, ra3, rb1, sb, rb2, rb3, acc_a, acc_b, sum_a, send_sem, recv_sem, load_sem):
    loads = [pltpu.make_async_copy(partials_hbm.at[i], partials.at[i], load_sem.at[i]) for i in range(SLOTS)]
    stats = [pltpu.make_async_copy(src, dst, load_sem.at[SLOTS + i]) for i, (src, dst) in enumerate((
        (left_stat_hbm, left_stat), (right_stat_hbm, right_stat), (left_root_hbm, left_root), (right_root_hbm, right_root)))]
    for copy in loads:
        copy.start()
    x, yl, yh, z, c = position()
    dp, ow = lax.axis_index("dp"), lax.axis_index("owner")

    def owner(dz, dy, dc=0):
        return (((yh + dy) % 2) * ZS + (z + dz) % ZS) * 2 + (c + dc) % 2

    xp = (((x + 1) % XS) * 2 + yl, ow)
    xm = (((x + XS - 1) % XS) * 2 + yl, ow)
    yo = (x * 2 + 1 - yl, ow)
    zp, zm = (dp, owner(1, 0)), (dp, owner(3, 0))
    yp, co = (dp, owner(0, 1)), (dp, owner(0, 0, 1))
    greet((xp, xm, yo, zp, zm, yp, co))
    for copy in loads:
        copy.wait()
    go = Copies(send_sem, recv_sem)

    def block_of(dx, dy):
        slot = ((x + dx) % XS) * 2 + (yl + dy) % 2
        found = jnp.int32(0)
        for r in range(SLOTS):
            found = jnp.where(owner_slot[ow, r] == slot, jnp.int32(r), found)
        return found

    where = {(dx, dy): block_of(dx, dy) for dx in range(XS) for dy in range(2)}

    def stage(dx, dy, rows):
        st[dx * 2 + dy, rows, :] = partials[where[dx, dy], rows, :]

    def own(dx, dy, rows):
        return st.at[dx * 2 + dy, rows]

    def first_a(dy):
        stage(2, dy, A_ALL)
        go.start(("a1p", dy), own(2, dy, A_LO), ra1.at[0, dy], xp)
        go.start(("a1m", dy), own(2, dy, A_HI), ra1.at[1, dy], xm)

    def own_a(dy):
        stage(1, dy, A_ALL)
        go.start(("a2p", dy), own(1, dy, A_HI), ra2.at[0, dy, HI_A], xp)
        stage(3, dy, A_ALL)
        go.start(("a2m", dy), own(3, dy, A_LO), ra2.at[1, dy, LO_A], xm)

    def sum_of_a(dy):
        go.arrived(("a1p", dy), ("a1m", dy))
        acc_a[0, dy] = (st[2 + dy, A_LO, :].astype(f32) + ra1[0, dy].astype(f32)).astype(bf16)
        go.start(("a3p", dy), acc_a.at[0, dy], ra2.at[0, dy, LO_A], xp)
        acc_a[1, dy] = (st[6 + dy, A_HI, :].astype(f32) + ra1[1, dy].astype(f32)).astype(bf16)
        go.start(("a3m", dy), acc_a.at[1, dy], ra2.at[1, dy, HI_A], xm)

    def first_b(dx):
        stage(dx, 1, B_ALL)
        go.start(("b1", dx), own(dx, 1, B_ALL), rb1.at[dx], yo)

    def sum_of_b(dx):
        stage(dx, 0, B_ALL)
        go.arrived(("b1", dx))
        sb[dx] = (st[dx * 2, B_ALL, :].astype(f32) + rb1[dx].astype(f32)).astype(bf16)

    first_a(1)
    for copy in stats:
        copy.start()
    first_b(2)
    first_a(0)
    own_a(1)
    first_b(1)
    stage(0, 0, A_ALL)
    stage(0, 1, A_ALL)
    sum_of_a(1)
    sum_of_b(2)
    first_b(3)
    own_a(0)
    sum_of_a(0)
    go.start("b2p", sb.at[2, LO_B], rb2.at[0], xp)
    go.start("b2m", sb.at[2, HI_B], rb2.at[1], xm)
    sum_of_b(1)
    first_b(0)
    go.start("b3p", sb.at[1, HI_B], rb3.at[0, HI_B], xp)
    go.arrived(("a2p", 1), ("a2m", 1), ("a3p", 1), ("a3m", 1))
    sum_a[...] = (st[1, A_ALL, :].astype(f32) + ra2[0, 1].astype(f32) + ra2[1, 1].astype(f32)).astype(bf16)
    go.start("a4", sum_a, ra3, yo)
    sum_of_b(3)
    go.start("b3m", sb.at[3, LO_B], rb3.at[1, LO_B], xm)
    go.arrived("b2p", "b2m")
    acc_b[0] = (sb[1, LO_B, :].astype(f32) + rb2[0].astype(f32)).astype(bf16)
    go.start("b4p", acc_b.at[0], rb3.at[0, LO_B], xp)
    acc_b[1] = (sb[3, HI_B, :].astype(f32) + rb2[1].astype(f32)).astype(bf16)
    go.start("b4m", acc_b.at[1], rb3.at[1, HI_B], xm)
    go.arrived(("a2p", 0), ("a2m", 0), ("a3p", 0), ("a3m", 0))
    stage(0, 0, B_ALL)
    go.arrived(("b1", 0))
    go.arrived("a4")
    g[A_ALL, :] = (st[0, A_ALL, :].astype(f32) + ra2[0, 0].astype(f32) + ra2[1, 0].astype(f32)
                       + ra3[...].astype(f32)).astype(bf16)
    go.arrived("b3p", "b3m", "b4p", "b4m")
    g[B_ALL, :] = (st[0, B_ALL, :].astype(f32) + rb1[0].astype(f32) + rb3[0].astype(f32)
                       + rb3[1].astype(f32)).astype(bf16)

    block = ow * SLOTS
    for r in range(SLOTS):
        block = jnp.where(owner_slot[ow, r] == dp, ow * SLOTS + r, block)
    hits = jnp.int32(0)
    for i in range(REFRESH):
        hits = hits + jnp.where(refresh[i] == block, jnp.int32(1), jnp.int32(0))
    for copy in stats:
        copy.wait()
    low = g[...]
    low_t = low.T
    weight = (1.0 - decay_rate) / N
    left_new[...] = decay_rate * left_stat[...] + weight * dot(low, low_t)
    right_new[...] = decay_rate * right_stat[...] + weight * dot(low_t, low)
    left_out[...] = jnp.where(hits > 0, root(left_new[...]), left_root[...].astype(f32)).astype(bf16)
    right_out[...] = jnp.where(hits > 0, root(right_new[...]), right_root[...].astype(f32)).astype(bf16)
    raw = dot(dot(left_out[...], low).astype(bf16), right_out[...])
    full = low.astype(f32)
    graft = jnp.sqrt(total(full * full) * (1.0 / (N * N))) / jnp.sqrt(total(raw * raw) * (1.0 / (N * N)) + graft_eps)
    update[...] = (raw * graft).astype(bf16)

    def pass_on(name, dz, dy, rows, target):
        piece = out.at[owner(dz, dy), rows]
        go.start(name, piece, piece, target)

    def share(dz, dy, rows, tag):
        pass_on(("core", dz, dy, tag), dz, dy, rows, co)

    def mine(name, rows, target):
        go.start(name, update.at[rows], out.at[owner(0, 0), rows], target)

    mine("yY", Y_ALL, yp)
    mine("zZ+", Z_ALL, zp)
    mine("zZ-", Z_ALL, zm)
    mine("zY+", Y_ALL, zp)
    mine("zY-", Y_ALL, zm)
    mine("yZ", Z_ALL, yp)
    mine("core", pl.ds(0, N), co)
    out[owner(0, 0)] = update[...]

    go.arrived("zZ+")
    pass_on("zZ2+", 3, 0, Z_LO, zp)
    pass_on("yZ-", 3, 0, Z_ALL, yp)
    share(3, 0, Z_ALL, "Z")
    go.arrived("zZ-")
    pass_on("zZ2-", 1, 0, Z_HI, zm)
    pass_on("yZ+", 1, 0, Z_ALL, yp)
    share(1, 0, Z_ALL, "Z")
    go.arrived("yY")
    pass_on("pY+", 0, 1, Y_ALL, zp)
    pass_on("pY-", 0, 1, Y_ALL, zm)
    share(0, 1, Y_ALL, "Y")
    go.arrived("zY+")
    pass_on("zY2+", 3, 0, Y_LO, zp)
    share(3, 0, Y_ALL, "Y")
    go.arrived("zY-")
    pass_on("zY2-", 1, 0, Y_HI, zm)
    share(1, 0, Y_ALL, "Y")
    go.arrived("yZ")
    share(0, 1, Z_ALL, "Z")
    go.arrived("zZ2+", "zZ2-")
    pass_on("yZ2", 2, 0, Z_ALL, yp)
    share(2, 0, Z_ALL, "Z")
    go.arrived("yZ-")
    share(3, 1, Z_ALL, "Z")
    go.arrived("pY+")
    pass_on("pY2+", 3, 1, Y_LO, zp)
    share(3, 1, Y_ALL, "Y")
    go.arrived("pY-")
    pass_on("pY2-", 1, 1, Y_HI, zm)
    share(1, 1, Y_ALL, "Y")
    go.arrived("yZ+")
    share(1, 1, Z_ALL, "Z")
    go.arrived("zY2+", "zY2-")
    share(2, 0, Y_ALL, "Y")
    go.arrived("yZ2")
    share(2, 1, Z_ALL, "Z")
    go.arrived("pY2+", "pY2-")
    share(2, 1, Y_ALL, "Y")
    go.arrived("core", *[name for name in go.started if name[0] == "core" and len(name) == 4 and name != "core"])
    go.finish()


def whole_step(*arrays):
    vmem, smem, hbm = (pl.BlockSpec(memory_space=space) for space in (pltpu.VMEM, pltpu.SMEM, pltpu.HBM))
    like = lambda dtype, *lead: pltpu.VMEM(lead + (N, N), dtype)
    vm = lambda *shape: pltpu.VMEM(shape + (N,), bf16)
    copies = 23 + 33
    return pl.pallas_call(
        step_kernel,
        out_shape=(like(bf16, 16), like(f32), like(f32), like(bf16), like(bf16)),
        in_specs=[smem] * 2 + [hbm] * 5,
        out_specs=[vmem] * 5,
        scratch_shapes=[
            vm(SLOTS, N), pltpu.VMEM((N, N), f32), pltpu.VMEM((N, N), f32), vm(N), vm(N), vm(N), vm(N),
            vm(SLOTS, N), vm(2, 2, RAH), vm(2, 2, RA), vm(RA), vm(XS, RB), vm(XS, RB), vm(2, RBH), vm(2, RB),
            vm(2, 2, RAH), vm(2, RBH), vm(RA),
            pltpu.SemaphoreType.DMA((copies,)), pltpu.SemaphoreType.DMA((copies,)), pltpu.SemaphoreType.DMA((SLOTS + 4,)),
        ],
        compiler_params=pltpu.CompilerParams(collective_id=0, has_side_effects=True, vmem_limit_bytes=44 * 2**20),
        name="whole_step",
    )(*arrays)


def write_kernel(*refs):
    count = len(refs) // 2
    sems = refs[-1]
    copies, at = [], 0
    for src, dst in zip(refs[:count], refs[count:-1]):
        parts = [(src.at[i], dst.at[i]) for i in range(src.shape[0])] if len(src.shape) == 3 else [(src, dst)]
        for part in parts:
            copies.append(pltpu.make_async_copy(*part, sems.at[at]))
            copies[-1].start()
            at += 1
    for copy in copies:
        copy.wait()


def write_out(arrays):
    return pl.pallas_call(
        write_kernel,
        out_shape=tuple(jax.ShapeDtypeStruct(a.shape, a.dtype) for a in arrays),
        in_specs=[pl.BlockSpec(memory_space=pltpu.VMEM)] * len(arrays),
        out_specs=[pl.BlockSpec(memory_space=pl.ANY)] * len(arrays),
        scratch_shapes=[pltpu.SemaphoreType.DMA((20,))],
        compiler_params=pltpu.CompilerParams(vmem_limit_bytes=2**20),
        name="write_out",
    )(*arrays)


def body(grad_partials, owner_slot, refresh_blocks, left_stat, right_stat, left_root, right_root):
    results = whole_step(owner_slot, refresh_blocks, grad_partials[0], left_stat[0, 0], right_stat[0, 0], left_root[0, 0], right_root[0, 0])
    update, *own = write_out(results)
    return (update[:, None], *(array[None, None] for array in own))


def solution(mesh):
    slots = P("owner", "dp", None, None)
    return jax.shard_map(
        body,
        mesh=mesh,
        in_specs=(P("dp", "owner", None, None), P(), P(), slots, slots, slots, slots),
        out_specs=(P(None, "dp", None, None), slots, slots, slots, slots),
        check_vma=False,
    )
```

time: 103 us -> 87.6 us (0.85)
  local copies, waits for them, and re-layouts: 18.9 us -> 1.36 us
  Pallas kernels: 83.2 us -> 85.4 us
    unnamed x16 -> x1, local copies, waits for them, and re-layouts: 18.9 us -> 1.36 us
    pallas_call x3 -> x2, Pallas kernels: 83.2 us -> 85.4 us  [the longest x1 81 us: whole_step(): pl.pallas_call(step_kernel, out_shape=(like(bf16, 16), like(f32), like(f3...]
where the time goes in v1:
time: 87.6 us; the launch traced here: 87.4 us
  Pallas kernels  85.4 us (97%)
  local copies, waits for them, and re-layouts  1.36 us (2%)
    pallas_call x1, Pallas kernels, whole_step(): pl.pallas_call(step_kernel, out_shape=(like(bf16, 16), like(f32), like(f3...  81 us
    pallas_call x1, Pallas kernels, write_out(): pl.pallas_call(write_kernel, out_shape=tuple((jax.ShapeDtypeStruct(a.shap...  4.4 us

profile of v1, /device:TPU:1, one launch (start us, length us, event | category | flops | bytes accessed | tf_op | source)
XLA Modules:
  0.0 87.4 jit_solution(11490122756368122108)
XLA Ops:
  0.6 1.4 %copy.12.owner_slot = s32[16,8]{1,0:T(8,128)} copy(s32[16,8]{0,1:T(8,128)} %param.8) | data formatting | bytes 1024 | tf_op args[1]
  2.0 81.0 %whole_step.1 = (bf16[16,512,512]{2,1,0:T(8,128)(2,1)S(1)}, f32[512,512]{1,0:T(8,128)S(1)}, f32[512,512]{1,0:T(8,128)S(1)}, bf16[512,512]{1,0:T(8,128)(2,1)S(1)}, bf16[512,512]{1,0:T(8,128)(2,1)S(1)}) custom-call(s32[16,8]{1,0:T(8,128)} %copy.12.owner_slot, s32[32]{0:T(128)} %refresh.1, bf16[8,512,512]{2,1,0:T(8,128)(2,1)} %bitcast.12, f32[512,512]{1,0:T(8,128)} %bitcast.13, ...), custom_call_target="tpu_custom_call" | custom-call | tf_op jit(solution)/shard_map/whole_step/pallas_call | solution.py:295
  83.0 4.4 %write_out.1 = (bf16[16,512,512]{2,1,0:T(8,128)(2,1)}, f32[512,512]{1,0:T(8,128)}, f32[512,512]{1,0:T(8,128)}, bf16[512,512]{1,0:T(8,128)(2,1)}, bf16[512,512]{1,0:T(8,128)(2,1)}) custom-call(bf16[16,512,512]{2,1,0:T(8,128)(2,1)S(1)} %get-tuple-element.15.refs_0_, f32[512,512]{1,0:T(8,128)S(1)} %get-tuple-element.16.refs_1_, ...), custom_call_target="tpu_custom_call" | custom-call | tf_op jit(solution)/shard_map/write_out/pallas_call | solution.py:326

commit v2 on v1

--- a/solution.py
+++ b/solution.py
@@ -11,6 +11,7 @@
 
 N = 512
 XS, ZS, SLOTS, REFRESH = 4, 4, 8, 32
+ITERS = 4
 decay_rate = 0.8
 graft_eps = 1e-06
 
@@ -74,35 +75,50 @@
     return jnp.sum(jnp.sum(a, axis=0, keepdims=True), axis=1, keepdims=True)
 
 
-def root(stat):
+def roots(stats, keep, kept, outs, d, q, u, hb, h, w, wide, tall):
     rows = lax.broadcasted_iota(jnp.int32, (N, N), 0)
     cols = lax.broadcasted_iota(jnp.int32, (N, N), 1)
-    eye = jnp.where(rows == cols, 1.0, 0.0).astype(f32)
-    scale = total(stat * eye) * (2.0 / N)
-    d = (eye - stat * (1.0 / scale)) * 0.25
-    h = eye + d
-    dh, dl = split(d)
-    d2 = dot(dh, dh) + (dot(dh, dl) + dot(dl, dh))
-    d2h, d2l = split(d2)
-    d3 = dot(dh, d2h) + (dot(dh, d2l) + dot(dl, d2h))
-    uh, ul = split(3.75 * d2 + d3)
-    d = 2.5 * d2 + 5.0 * d3 + (dot(d2h, uh) + (dot(d2h, ul) + dot(d2l, uh)))
-    for sweep in range(3):
-        low = d.astype(bf16)
-        h = h + dot(h.astype(bf16), low)
-        if sweep == 2:
+    both = range(2)
+    final = []
+    for m in both:
+        eye = jnp.where(rows == cols, 1.0, 0.0).astype(f32)
+        stat = stats[m][...]
+        scale = total(stat * eye) * (2.0 / N)
+        final.append(lax.rsqrt(jnp.sqrt(scale)))
+        first = (eye - stat * (1.0 / scale)) * 0.25
+        high, rest = split(first)
+        d[m] = high
+        h[m] = eye + first
+        hb[m] = (eye + first).astype(bf16)
+        wide[m, :, 0:N], wide[m, :, N:2 * N], wide[m, :, 2 * N:3 * N] = high, high, rest
+        tall[m, 0:N, :], tall[m, N:2 * N, :], tall[m, 2 * N:3 * N, :] = high, rest, high
+    for sweep in range(ITERS):
+        for m in both:
+            if sweep > 0:
+                new = h[m] + dot(hb[m], d[m])
+                if sweep == ITERS - 1:
+                    outs[m][...] = jnp.where(keep, kept[m][...], (new * final[m]).astype(bf16))
+                    continue
+                h[m] = new
+                hb[m] = new.astype(bf16)
+            square = dot(d[m], d[m]) if sweep > 0 else dot(wide[m], tall[m])
+            w[m] = square
+            q[m] = square.astype(bf16)
+        if sweep == ITERS - 1:
             break
-        d2 = dot(low, low)
-        d2h = d2.astype(bf16)
-        d3 = dot(low, d2h)
-        d = 2.5 * d2 + 5.0 * d3 + dot(d2h, (3.75 * d2 + d3).astype(bf16))
-    return h * lax.rsqrt(jnp.sqrt(scale))
+        for m in both:
+            cube = dot(d[m], q[m])
+            square = w[m]
+            u[m] = (3.75 * square + cube).astype(bf16)
+            w[m] = 2.5 * square + 5.0 * cube
+        for m in both:
+            d[m] = (w[m] + dot(q[m], u[m])).astype(bf16)
 
 
 def step_kernel(owner_slot, refresh, partials_hbm, left_stat_hbm, right_stat_hbm, left_root_hbm, right_root_hbm,
                 out, left_new, right_new, left_out, right_out,
                 partials, left_stat, right_stat, left_root, right_root, g, update,
-                st, ra1, ra2, ra3, rb1, sb, rb2, rb3, acc_a, acc_b, sum_a, send_sem, recv_sem, load_sem):
+                st, ra1, ra2, ra3, rb1, sb, rb2, rb3, acc_a, acc_b, sum_a, send_sem, recv_sem, load_sem, *root_scratch):
     loads = [pltpu.make_async_copy(partials_hbm.at[i], partials.at[i], load_sem.at[i]) for i in range(SLOTS)]
     stats = [pltpu.make_async_copy(src, dst, load_sem.at[SLOTS + i]) for i, (src, dst) in enumerate((
         (left_stat_hbm, left_stat), (right_stat_hbm, right_stat), (left_root_hbm, left_root), (right_root_hbm, right_root)))]
@@ -128,7 +144,7 @@
         slot = ((x + dx) % XS) * 2 + (yl + dy) % 2
         found = jnp.int32(0)
         for r in range(SLOTS):
-            found = jnp.where(owner_slot[ow, r] == slot, jnp.int32(r), found)
+            found = jnp.where(owner_slot[r, ow] == slot, jnp.int32(r), found)
         return found
 
     where = {(dx, dy): block_of(dx, dy) for dx in range(XS) for dy in range(2)}
@@ -207,7 +223,7 @@
 
     block = ow * SLOTS
     for r in range(SLOTS):
-        block = jnp.where(owner_slot[ow, r] == dp, ow * SLOTS + r, block)
+        block = jnp.where(owner_slot[r, ow] == dp, ow * SLOTS + r, block)
     hits = jnp.int32(0)
     for i in range(REFRESH):
         hits = hits + jnp.where(refresh[i] == block, jnp.int32(1), jnp.int32(0))
@@ -218,8 +234,7 @@
     weight = (1.0 - decay_rate) / N
     left_new[...] = decay_rate * left_stat[...] + weight * dot(low, low_t)
     right_new[...] = decay_rate * right_stat[...] + weight * dot(low_t, low)
-    left_out[...] = jnp.where(hits > 0, root(left_new[...]), left_root[...].astype(f32)).astype(bf16)
-    right_out[...] = jnp.where(hits > 0, root(right_new[...]), right_root[...].astype(f32)).astype(bf16)
+    roots((left_new, right_new), hits == 0, (left_root, right_root), (left_out, right_out), *root_scratch)
     raw = dot(dot(left_out[...], low).astype(bf16), right_out[...])
     full = low.astype(f32)
     graft = jnp.sqrt(total(full * full) * (1.0 / (N * N))) / jnp.sqrt(total(raw * raw) * (1.0 / (N * N)) + graft_eps)
@@ -302,6 +317,8 @@
             vm(SLOTS, N), vm(2, 2, RAH), vm(2, 2, RA), vm(RA), vm(XS, RB), vm(XS, RB), vm(2, RBH), vm(2, RB),
             vm(2, 2, RAH), vm(2, RBH), vm(RA),
             pltpu.SemaphoreType.DMA((copies,)), pltpu.SemaphoreType.DMA((copies,)), pltpu.SemaphoreType.DMA((SLOTS + 4,)),
+            *[pltpu.VMEM((2, N, N), dtype) for dtype in (bf16, bf16, bf16, bf16, f32, f32)],
+            pltpu.VMEM((2, N, 3 * N), bf16), pltpu.VMEM((2, 3 * N, N), bf16),
         ],
         compiler_params=pltpu.CompilerParams(collective_id=0, has_side_effects=True, vmem_limit_bytes=44 * 2**20),
         name="whole_step",
@@ -335,7 +352,7 @@
 
 
 def body(grad_partials, owner_slot, refresh_blocks, left_stat, right_stat, left_root, right_root):
-    results = whole_step(owner_slot, refresh_blocks, grad_partials[0], left_stat[0, 0], right_stat[0, 0], left_root[0, 0], right_root[0, 0])
+    results = whole_step(owner_slot.T, refresh_blocks, grad_partials[0], left_stat[0, 0], right_stat[0, 0], left_root[0, 0], right_root[0, 0])
     update, *own = write_out(results)
     return (update[:, None], *(array[None, None] for array in own))
 

time: 87.6 us -> 83.2 us (0.950)
  Pallas kernels: 85.4 us -> 82.4 us
  local copies, waits for them, and re-layouts: 1.36 us -> 0 us
    pallas_call x1, Pallas kernels: 81 us -> 78 us  [whole_step(): pl.pallas_call(step_kernel, out_shape=(like(bf16, 16), like(f32), like(f3...]
    unnamed x1 -> x0, local copies, waits for them, and re-layouts: 1.36 us -> none
where the time goes in v2:
time: 83.2 us; the launch traced here: 83 us
  Pallas kernels  82.4 us (99%)
    pallas_call x1, Pallas kernels, whole_step(): pl.pallas_call(step_kernel, out_shape=(like(bf16, 16), like(f32), like(f3...  78 us
    pallas_call x1, Pallas kernels, write_out(): pl.pallas_call(write_kernel, out_shape=tuple((jax.ShapeDtypeStruct(a.shap...  4.4 us

profile of v2, /device:TPU:1, one launch (start us, length us, event | category | flops | bytes accessed | tf_op | source)
XLA Modules:
  0.0 83.0 jit_solution(5753990671861967249)
XLA Ops:
  0.6 78.0 %whole_step.1 = (bf16[16,512,512]{2,1,0:T(8,128)(2,1)S(1)}, f32[512,512]{1,0:T(8,128)S(1)}, f32[512,512]{1,0:T(8,128)S(1)}, bf16[512,512]{1,0:T(8,128)(2,1)S(1)}, bf16[512,512]{1,0:T(8,128)(2,1)S(1)}) custom-call(s32[8,16]{1,0:T(8,128)} %bitcast.18, s32[32]{0:T(128)} %refresh.1, bf16[8,512,512]{2,1,0:T(8,128)(2,1)} %bitcast.13, f32[512,512]{1,0:T(8,128)} %bitcast.14, ...), custom_call_target="tpu_custom_call" | custom-call | tf_op jit(solution)/shard_map/whole_step/pallas_call | solution.py:310
  78.6 4.4 %write_out.1 = (bf16[16,512,512]{2,1,0:T(8,128)(2,1)}, f32[512,512]{1,0:T(8,128)}, f32[512,512]{1,0:T(8,128)}, bf16[512,512]{1,0:T(8,128)(2,1)}, bf16[512,512]{1,0:T(8,128)(2,1)}) custom-call(bf16[16,512,512]{2,1,0:T(8,128)(2,1)S(1)} %get-tuple-element.15.refs_0_, f32[512,512]{1,0:T(8,128)S(1)} %get-tuple-element.16.refs_1_, ...), custom_call_target="tpu_custom_call" | custom-call | tf_op jit(solution)/shard_map/write_out/pallas_call | solution.py:343

commit v3 on v2

--- a/solution.py
+++ b/solution.py
@@ -75,7 +75,7 @@
     return jnp.sum(jnp.sum(a, axis=0, keepdims=True), axis=1, keepdims=True)
 
 
-def roots(stats, keep, kept, outs, d, q, u, hb, h, w, wide, tall):
+def roots(stats, outs, d, q, u, hb, h, w, wide, tall):
     rows = lax.broadcasted_iota(jnp.int32, (N, N), 0)
     cols = lax.broadcasted_iota(jnp.int32, (N, N), 1)
     both = range(2)
@@ -97,7 +97,7 @@
             if sweep > 0:
                 new = h[m] + dot(hb[m], d[m])
                 if sweep == ITERS - 1:
-                    outs[m][...] = jnp.where(keep, kept[m][...], (new * final[m]).astype(bf16))
+                    outs[m][...] = (new * final[m]).astype(bf16)
                     continue
                 h[m] = new
                 hb[m] = new.astype(bf16)
@@ -115,10 +115,9 @@
             d[m] = (w[m] + dot(q[m], u[m])).astype(bf16)
 
 
-def step_kernel(owner_slot, refresh, partials_hbm, left_stat_hbm, right_stat_hbm, left_root_hbm, right_root_hbm,
-                out, left_new, right_new, left_out, right_out,
-                partials, left_stat, right_stat, left_root, right_root, g, update,
-                st, ra1, ra2, ra3, rb1, sb, rb2, rb3, acc_a, acc_b, sum_a, send_sem, recv_sem, load_sem, *root_scratch):
+def reduce_kernel(owner_slot, partials_hbm, left_stat_hbm, right_stat_hbm, left_root_hbm, right_root_hbm,
+                  g, left_stat, right_stat, left_root, right_root,
+                  partials, st, ra1, ra2, ra3, rb1, sb, rb2, rb3, acc_a, acc_b, sum_a, send_sem, recv_sem, load_sem):
     loads = [pltpu.make_async_copy(partials_hbm.at[i], partials.at[i], load_sem.at[i]) for i in range(SLOTS)]
     stats = [pltpu.make_async_copy(src, dst, load_sem.at[SLOTS + i]) for i, (src, dst) in enumerate((
         (left_stat_hbm, left_stat), (right_stat_hbm, right_stat), (left_root_hbm, left_root), (right_root_hbm, right_root)))]
@@ -126,16 +125,10 @@
         copy.start()
     x, yl, yh, z, c = position()
     dp, ow = lax.axis_index("dp"), lax.axis_index("owner")
-
-    def owner(dz, dy, dc=0):
-        return (((yh + dy) % 2) * ZS + (z + dz) % ZS) * 2 + (c + dc) % 2
-
     xp = (((x + 1) % XS) * 2 + yl, ow)
     xm = (((x + XS - 1) % XS) * 2 + yl, ow)
     yo = (x * 2 + 1 - yl, ow)
-    zp, zm = (dp, owner(1, 0)), (dp, owner(3, 0))
-    yp, co = (dp, owner(0, 1)), (dp, owner(0, 0, 1))
-    greet((xp, xm, yo, zp, zm, yp, co))
+    greet((xp, xm, yo))
     for copy in loads:
         copy.wait()
     go = Copies(send_sem, recv_sem)
@@ -152,19 +145,19 @@
     def stage(dx, dy, rows):
         st[dx * 2 + dy, rows, :] = partials[where[dx, dy], rows, :]
 
-    def own(dx, dy, rows):
+    def part(dx, dy, rows):
         return st.at[dx * 2 + dy, rows]
 
     def first_a(dy):
         stage(2, dy, A_ALL)
-        go.start(("a1p", dy), own(2, dy, A_LO), ra1.at[0, dy], xp)
-        go.start(("a1m", dy), own(2, dy, A_HI), ra1.at[1, dy], xm)
+        go.start(("a1p", dy), part(2, dy, A_LO), ra1.at[0, dy], xp)
+        go.start(("a1m", dy), part(2, dy, A_HI), ra1.at[1, dy], xm)
 
     def own_a(dy):
         stage(1, dy, A_ALL)
-        go.start(("a2p", dy), own(1, dy, A_HI), ra2.at[0, dy, HI_A], xp)
+        go.start(("a2p", dy), part(1, dy, A_HI), ra2.at[0, dy, HI_A], xp)
         stage(3, dy, A_ALL)
-        go.start(("a2m", dy), own(3, dy, A_LO), ra2.at[1, dy, LO_A], xm)
+        go.start(("a2m", dy), part(3, dy, A_LO), ra2.at[1, dy, LO_A], xm)
 
     def sum_of_a(dy):
         go.arrived(("a1p", dy), ("a1m", dy))
@@ -175,7 +168,7 @@
 
     def first_b(dx):
         stage(dx, 1, B_ALL)
-        go.start(("b1", dx), own(dx, 1, B_ALL), rb1.at[dx], yo)
+        go.start(("b1", dx), part(dx, 1, B_ALL), rb1.at[dx], yo)
 
     def sum_of_b(dx):
         stage(dx, 0, B_ALL)
@@ -220,25 +213,100 @@
     go.arrived("b3p", "b3m", "b4p", "b4m")
     g[B_ALL, :] = (st[0, B_ALL, :].astype(f32) + rb1[0].astype(f32) + rb3[0].astype(f32)
                        + rb3[1].astype(f32)).astype(bf16)
-
+    for copy in stats:
+        copy.wait()
+    go.finish()
+
+
+vmem, smem, hbm = (pl.BlockSpec(memory_space=space) for space in (pltpu.VMEM, pltpu.SMEM, pltpu.HBM))
+
+
+def own(space, dtype, *lead):
+    return space(lead + (N, N), dtype)
+
+
+def reduce_scatter(*arrays):
+    vm = lambda *shape: pltpu.VMEM(shape + (N,), bf16)
+    return pl.pallas_call(
+        reduce_kernel,
+        out_shape=tuple(own(pltpu.VMEM, dtype) for dtype in (bf16, f32, f32, bf16, bf16)),
+        in_specs=[smem] + [hbm] * 5,
+        out_specs=[vmem] * 5,
+        scratch_shapes=[
+            vm(SLOTS, N), vm(SLOTS, N), vm(2, 2, RAH), vm(2, 2, RA), vm(RA), vm(XS, RB), vm(XS, RB), vm(2, RBH), vm(2, RB),
+            vm(2, 2, RAH), vm(2, RBH), vm(RA),
+            pltpu.SemaphoreType.DMA((23,)), pltpu.SemaphoreType.DMA((23,)), pltpu.SemaphoreType.DMA((SLOTS + 4,)),
+        ],
+        compiler_params=pltpu.CompilerParams(collective_id=0, has_side_effects=True, vmem_limit_bytes=24 * 2**20),
+        name="reduce_scatter",
+    )(*arrays)
+
+
+def local_kernel(owner_slot, refresh, g, left_stat, right_stat, left_root, right_root,
+                 update, left_new_hbm, right_new_hbm, left_out_hbm, right_out_hbm,
+                 left_new, right_new, left_out, right_out, sems, *root_scratch):
+    dp, ow = lax.axis_index("dp"), lax.axis_index("owner")
+    writes = [pltpu.make_async_copy(src, dst, sems.at[i]) for i, (src, dst) in enumerate((
+        (left_new, left_new_hbm), (right_new, right_new_hbm), (left_out, left_out_hbm), (right_out, right_out_hbm)))]
     block = ow * SLOTS
     for r in range(SLOTS):
         block = jnp.where(owner_slot[r, ow] == dp, ow * SLOTS + r, block)
     hits = jnp.int32(0)
     for i in range(REFRESH):
         hits = hits + jnp.where(refresh[i] == block, jnp.int32(1), jnp.int32(0))
-    for copy in stats:
-        copy.wait()
     low = g[...]
     low_t = low.T
     weight = (1.0 - decay_rate) / N
     left_new[...] = decay_rate * left_stat[...] + weight * dot(low, low_t)
     right_new[...] = decay_rate * right_stat[...] + weight * dot(low_t, low)
-    roots((left_new, right_new), hits == 0, (left_root, right_root), (left_out, right_out), *root_scratch)
+    writes[0].start()
+    writes[1].start()
+
+    @pl.when(hits > 0)
+    def _():
+        roots((left_new, right_new), (left_out, right_out), *root_scratch)
+
+    @pl.when(hits == 0)
+    def _():
+        left_out[...] = left_root[...]
+        right_out[...] = right_root[...]
+
+    writes[2].start()
+    writes[3].start()
     raw = dot(dot(left_out[...], low).astype(bf16), right_out[...])
     full = low.astype(f32)
     graft = jnp.sqrt(total(full * full) * (1.0 / (N * N))) / jnp.sqrt(total(raw * raw) * (1.0 / (N * N)) + graft_eps)
     update[...] = (raw * graft).astype(bf16)
+    for copy in writes:
+        copy.wait()
+
+
+def local_step(*arrays):
+    mine = (bf16, f32, f32, bf16, bf16)
+    return pl.pallas_call(
+        local_kernel,
+        out_shape=(own(pltpu.VMEM, bf16),) + tuple(own(pltpu.HBM, dtype) for dtype in mine[1:]),
+        in_specs=[smem] * 2 + [vmem] * 5,
+        out_specs=[vmem] + [hbm] * 4,
+        scratch_shapes=[own(pltpu.VMEM, dtype) for dtype in mine[1:]] + [pltpu.SemaphoreType.DMA((4,))]
+        + [own(pltpu.VMEM, dtype, 2) for dtype in (bf16, bf16, bf16, bf16, f32, f32)]
+        + [pltpu.VMEM((2, N, 3 * N), bf16), pltpu.VMEM((2, 3 * N, N), bf16)],
+        compiler_params=pltpu.CompilerParams(vmem_limit_bytes=32 * 2**20),
+        name="local_step",
+    )(*arrays)
+
+
+def gather_kernel(update, out, send_sem, recv_sem):
+    x, yl, yh, z, c = position()
+    dp, ow = lax.axis_index("dp"), lax.axis_index("owner")
+
+    def owner(dz, dy, dc=0):
+        return (((yh + dy) % 2) * ZS + (z + dz) % ZS) * 2 + (c + dc) % 2
+
+    zp, zm = (dp, owner(1, 0)), (dp, owner(3, 0))
+    yp, co = (dp, owner(0, 1)), (dp, owner(0, 0, 1))
+    greet((zp, zm, yp, co))
+    go = Copies(send_sem, recv_sem)
 
     def pass_on(name, dz, dy, rows, target):
         piece = out.at[owner(dz, dy), rows]
@@ -302,59 +370,44 @@
     go.finish()
 
 
-def whole_step(*arrays):
-    vmem, smem, hbm = (pl.BlockSpec(memory_space=space) for space in (pltpu.VMEM, pltpu.SMEM, pltpu.HBM))
-    like = lambda dtype, *lead: pltpu.VMEM(lead + (N, N), dtype)
-    vm = lambda *shape: pltpu.VMEM(shape + (N,), bf16)
-    copies = 23 + 33
+def all_gather(update):
     return pl.pallas_call(
-        step_kernel,
-        out_shape=(like(bf16, 16), like(f32), like(f32), like(bf16), like(bf16)),
-        in_specs=[smem] * 2 + [hbm] * 5,
-        out_specs=[vmem] * 5,
-        scratch_shapes=[
-            vm(SLOTS, N), pltpu.VMEM((N, N), f32), pltpu.VMEM((N, N), f32), vm(N), vm(N), vm(N), vm(N),
-            vm(SLOTS, N), vm(2, 2, RAH), vm(2, 2, RA), vm(RA), vm(XS, RB), vm(XS, RB), vm(2, RBH), vm(2, RB),
-            vm(2, 2, RAH), vm(2, RBH), vm(RA),
-            pltpu.SemaphoreType.DMA((copies,)), pltpu.SemaphoreType.DMA((copies,)), pltpu.SemaphoreType.DMA((SLOTS + 4,)),
-            *[pltpu.VMEM((2, N, N), dtype) for dtype in (bf16, bf16, bf16, bf16, f32, f32)],
-            pltpu.VMEM((2, N, 3 * N), bf16), pltpu.VMEM((2, 3 * N, N), bf16),
-        ],
-        compiler_params=pltpu.CompilerParams(collective_id=0, has_side_effects=True, vmem_limit_bytes=44 * 2**20),
-        name="whole_step",
-    )(*arrays)
-
-
-def write_kernel(*refs):
-    count = len(refs) // 2
-    sems = refs[-1]
-    copies, at = [], 0
-    for src, dst in zip(refs[:count], refs[count:-1]):
-        parts = [(src.at[i], dst.at[i]) for i in range(src.shape[0])] if len(src.shape) == 3 else [(src, dst)]
-        for part in parts:
-            copies.append(pltpu.make_async_copy(*part, sems.at[at]))
-            copies[-1].start()
-            at += 1
+        gather_kernel,
+        out_shape=own(pltpu.VMEM, bf16, 16),
+        in_specs=[vmem],
+        out_specs=vmem,
+        scratch_shapes=[pltpu.SemaphoreType.DMA((33,)), pltpu.SemaphoreType.DMA((33,))],
+        compiler_params=pltpu.CompilerParams(collective_id=1, has_side_effects=True, vmem_limit_bytes=2 * 2**20),
+        name="all_gather",
+    )(update)
+
+
+def write_kernel(src, dst, sems):
+    copies = [pltpu.make_async_copy(src.at[i], dst.at[i], sems.at[i]) for i in range(16)]
+    for copy in copies:
+        copy.start()
     for copy in copies:
         copy.wait()
 
 
-def write_out(arrays):
+def write_out(gathered):
     return pl.pallas_call(
         write_kernel,
-        out_shape=tuple(jax.ShapeDtypeStruct(a.shape, a.dtype) for a in arrays),
-        in_specs=[pl.BlockSpec(memory_space=pltpu.VMEM)] * len(arrays),
-        out_specs=[pl.BlockSpec(memory_space=pl.ANY)] * len(arrays),
-        scratch_shapes=[pltpu.SemaphoreType.DMA((20,))],
+        out_shape=own(pltpu.HBM, bf16, 16),
+        in_specs=[vmem],
+        out_specs=hbm,
+        scratch_shapes=[pltpu.SemaphoreType.DMA((16,))],
         compiler_params=pltpu.CompilerParams(vmem_limit_bytes=2**20),
         name="write_out",
-    )(*arrays)
+    )(gathered)
 
 
 def body(grad_partials, owner_slot, refresh_blocks, left_stat, right_stat, left_root, right_root):
-    results = whole_step(owner_slot.T, refresh_blocks, grad_partials[0], left_stat[0, 0], right_stat[0, 0], left_root[0, 0], right_root[0, 0])
-    update, *own = write_out(results)
-    return (update[:, None], *(array[None, None] for array in own))
+    table = owner_slot.T
+    reduced = reduce_scatter(table, grad_partials[0], left_stat[0, 0], right_stat[0, 0], left_root[0, 0], right_root[0, 0])
+    update, *mine = local_step(table, refresh_blocks, *reduced)
+    gathered = write_out(all_gather(update))
+    return (gathered[:, None], *(array[None, None] for array in mine))
 
 
 def solution(mesh):

time: 83.2 us -> 93.2 us (1.12)
  local copies, waits for them, and re-layouts: 0 us -> 8.73 us
  Pallas kernels: 82.4 us -> 83.4 us
    unnamed x0 -> x16, local copies, waits for them, and re-layouts: none -> 8.73 us
    pallas_call x2 -> x4, Pallas kernels: 82.4 us -> 83.4 us  [the longest x1 44.4 us: all_gather(): pl.pallas_call(gather_kernel, out_shape=own(pltpu.VMEM, bf16, 16), in_spe...]
where the time goes in v3:
time: 93.2 us; the launch traced here: 92.8 us
  Pallas kernels  83.4 us (89%)
  local copies, waits for them, and re-layouts  8.73 us (9%)
    pallas_call x1, Pallas kernels, all_gather(): pl.pallas_call(gather_kernel, out_shape=own(pltpu.VMEM, bf16, 16), in_spe...  44.4 us
    pallas_call x1, Pallas kernels, reduce_scatter(): pl.pallas_call(reduce_kernel, out_shape=tuple((own(pltpu.VMEM, dtype) for...  32.7 us
    unnamed x16, local copies, waits for them, and re-layouts  8.73 us
    pallas_call x1, Pallas kernels, write_out(): pl.pallas_call(write_kernel, out_shape=own(pltpu.HBM, bf16, 16), in_specs...  3.42 us
    pallas_call x1, Pallas kernels, local_step(): pl.pallas_call(local_kernel, out_shape=(own(pltpu.VMEM, bf16),) + tuple((...  2.87 us

profile of v3, /device:TPU:1, one launch (start us, length us, event | category | flops | bytes accessed | tf_op | source)
XLA Modules:
  0.0 92.8 jit_solution(14346559295147453317)
XLA Ops:
  0.6 0.0 copy-start
  0.6 2.2 %copy-done = bf16[1,8,512,512]{3,2,1,0:T(8,128)(2,1)S(1)} copy-done((bf16[1,8,512,512]{3,2,1,0:T(8,128)(2,1)S(1)}, bf16[1,8,512,512]{3,2,1,0:T(8,128)(2,1)}, u32[]{:S(2)}) %copy-start) | copy-done | bytes 4194328
  2.8 0.0 copy-start.1
  2.8 1.2 %copy-done.1 = f32[1,1,512,512]{3,2,1,0:T(8,128)S(1)} copy-done((f32[1,1,512,512]{3,2,1,0:T(8,128)S(1)}, f32[1,1,512,512]{3,2,1,0:T(8,128)}, u32[]{:S(2)}) %copy-start.1) | copy-done | bytes 1048600
  4.0 0.0 copy-start.2
  4.0 1.2 %copy-done.2 = f32[1,1,512,512]{3,2,1,0:T(8,128)S(1)} copy-done((f32[1,1,512,512]{3,2,1,0:T(8,128)S(1)}, f32[1,1,512,512]{3,2,1,0:T(8,128)}, u32[]{:S(2)}) %copy-start.2) | copy-done | bytes 1048600
  5.3 0.0 copy-start.3
  5.3 1.0 %copy-done.3 = bf16[1,1,512,512]{3,2,1,0:T(8,128)(2,1)S(1)} copy-done((bf16[1,1,512,512]{3,2,1,0:T(8,128)(2,1)S(1)}, bf16[1,1,512,512]{3,2,1,0:T(8,128)(2,1)}, u32[]{:S(2)}) %copy-start.3) | copy-done | bytes 524312
  6.3 0.0 copy-start.4
  6.3 1.0 %copy-done.4 = bf16[1,1,512,512]{3,2,1,0:T(8,128)(2,1)S(1)} copy-done((bf16[1,1,512,512]{3,2,1,0:T(8,128)(2,1)S(1)}, bf16[1,1,512,512]{3,2,1,0:T(8,128)(2,1)}, u32[]{:S(2)}) %copy-start.4) | copy-done | bytes 524312
  7.4 0.0 copy-start.5
  7.4 0.7 copy-done.5
  8.0 32.7 %reduce_scatter.1 = (bf16[512,512]{1,0:T(8,128)(2,1)S(1)}, f32[512,512]{1,0:T(8,128)S(1)}, f32[512,512]{1,0:T(8,128)S(1)}, bf16[512,512]{1,0:T(8,128)(2,1)S(1)}, bf16[512,512]{1,0:T(8,128)(2,1)S(1)}) custom-call(s32[8,16]{1,0:T(8,128)S(1)} %bitcast.18, bf16[8,512,512]{2,1,0:T(8,128)(2,1)S(1)} %bitcast.13, f32[512,512]{1,0:T(8,128)S(1)} %bitcast.14, ...), custom_call_target="tpu_custom_call" | custom-call | tf_op jit(solution)/shard_map/reduce_scatter/pallas_call | solution.py:230
  40.7 0.0 copy-start.6
  40.7 0.7 copy-done.6
  41.4 0.0 copy-start.7
  41.4 0.7 copy-done.7
  42.1 2.9 %local_step.1 = (bf16[512,512]{1,0:T(8,128)(2,1)S(1)}, f32[512,512]{1,0:T(8,128)}, f32[512,512]{1,0:T(8,128)}, bf16[512,512]{1,0:T(8,128)(2,1)}, bf16[512,512]{1,0:T(8,128)(2,1)}) custom-call(s32[8,16]{1,0:T(8,128)S(1)} %bitcast.19, s32[32]{0:T(128)S(1)} %copy-done.7, bf16[512,512]{1,0:T(8,128)(2,1)S(1)} %get-tuple-element.15.g, ...), custom_call_target="tpu_custom_call" | custom-call | tf_op jit(solution)/shard_map/local_step/pallas_call | solution.py:286
  45.0 44.4 %all_gather.1.src = bf16[16,512,512]{2,1,0:T(8,128)(2,1)S(1)} custom-call(bf16[512,512]{1,0:T(8,128)(2,1)S(1)} %get-tuple-element.20.update), custom_call_target="tpu_custom_call" | custom-call | tf_op jit(solution)/shard_map/all_gather/pallas_call | solution.py:374
  89.4 3.4 %write_out.1 = bf16[16,512,512]{2,1,0:T(8,128)(2,1)} custom-call(bf16[16,512,512]{2,1,0:T(8,128)(2,1)S(1)} %all_gather.1.src), custom_call_target="tpu_custom_call" | custom-call | tf_op jit(solution)/shard_map/write_out/pallas_call | solution.py:394
Async XLA Ops:
  0.6 2.2 %copy-start = (bf16[1,8,512,512]{3,2,1,0:T(8,128)(2,1)S(1)}, bf16[1,8,512,512]{3,2,1,0:T(8,128)(2,1)}, u32[]{:S(2)}) copy-start(bf16[1,8,512,512]{3,2,1,0:T(8,128)(2,1)} %param.7) | copy-start | bytes 12582916
  2.8 1.2 %copy-start.1 = (f32[1,1,512,512]{3,2,1,0:T(8,128)S(1)}, f32[1,1,512,512]{3,2,1,0:T(8,128)}, u32[]{:S(2)}) copy-start(f32[1,1,512,512]{3,2,1,0:T(8,128)} %param.10) | copy-start | bytes 3145732
  4.0 1.2 %copy-start.2 = (f32[1,1,512,512]{3,2,1,0:T(8,128)S(1)}, f32[1,1,512,512]{3,2,1,0:T(8,128)}, u32[]{:S(2)}) copy-start(f32[1,1,512,512]{3,2,1,0:T(8,128)} %param.11) | copy-start | bytes 3145732
  5.3 1.0 %copy-start.3 = (bf16[1,1,512,512]{3,2,1,0:T(8,128)(2,1)S(1)}, bf16[1,1,512,512]{3,2,1,0:T(8,128)(2,1)}, u32[]{:S(2)}) copy-start(bf16[1,1,512,512]{3,2,1,0:T(8,128)(2,1)} %param.12) | copy-start | bytes 1572868
  6.3 1.0 %copy-start.4 = (bf16[1,1,512,512]{3,2,1,0:T(8,128)(2,1)S(1)}, bf16[1,1,512,512]{3,2,1,0:T(8,128)(2,1)}, u32[]{:S(2)}) copy-start(bf16[1,1,512,512]{3,2,1,0:T(8,128)(2,1)} %param.13) | copy-start | bytes 1572868
  7.4 0.7 copy-start.5
  40.7 0.7 copy-start.6
  41.4 0.7 copy-start.7

commit v4 on v3

--- a/solution.py
+++ b/solution.py
@@ -115,8 +115,8 @@
             d[m] = (w[m] + dot(q[m], u[m])).astype(bf16)
 
 
-def reduce_kernel(owner_slot, partials_hbm, left_stat_hbm, right_stat_hbm, left_root_hbm, right_root_hbm,
-                  g, left_stat, right_stat, left_root, right_root,
+def reduce_kernel(owner_slot, refresh, partials_hbm, left_stat_hbm, right_stat_hbm, left_root_hbm, right_root_hbm,
+                  hit, g, left_stat, right_stat, left_root, right_root,
                   partials, st, ra1, ra2, ra3, rb1, sb, rb2, rb3, acc_a, acc_b, sum_a, send_sem, recv_sem, load_sem):
     loads = [pltpu.make_async_copy(partials_hbm.at[i], partials.at[i], load_sem.at[i]) for i in range(SLOTS)]
     stats = [pltpu.make_async_copy(src, dst, load_sem.at[SLOTS + i]) for i, (src, dst) in enumerate((
@@ -213,47 +213,47 @@
     go.arrived("b3p", "b3m", "b4p", "b4m")
     g[B_ALL, :] = (st[0, B_ALL, :].astype(f32) + rb1[0].astype(f32) + rb3[0].astype(f32)
                        + rb3[1].astype(f32)).astype(bf16)
-    for copy in stats:
-        copy.wait()
-    go.finish()
-
-
-vmem, smem, hbm = (pl.BlockSpec(memory_space=space) for space in (pltpu.VMEM, pltpu.SMEM, pltpu.HBM))
-
-
-def own(space, dtype, *lead):
-    return space(lead + (N, N), dtype)
-
-
-def reduce_scatter(*arrays):
-    vm = lambda *shape: pltpu.VMEM(shape + (N,), bf16)
-    return pl.pallas_call(
-        reduce_kernel,
-        out_shape=tuple(own(pltpu.VMEM, dtype) for dtype in (bf16, f32, f32, bf16, bf16)),
-        in_specs=[smem] + [hbm] * 5,
-        out_specs=[vmem] * 5,
-        scratch_shapes=[
-            vm(SLOTS, N), vm(SLOTS, N), vm(2, 2, RAH), vm(2, 2, RA), vm(RA), vm(XS, RB), vm(XS, RB), vm(2, RBH), vm(2, RB),
-            vm(2, 2, RAH), vm(2, RBH), vm(RA),
-            pltpu.SemaphoreType.DMA((23,)), pltpu.SemaphoreType.DMA((23,)), pltpu.SemaphoreType.DMA((SLOTS + 4,)),
-        ],
-        compiler_params=pltpu.CompilerParams(collective_id=0, has_side_effects=True, vmem_limit_bytes=24 * 2**20),
-        name="reduce_scatter",
-    )(*arrays)
-
-
-def local_kernel(owner_slot, refresh, g, left_stat, right_stat, left_root, right_root,
-                 update, left_new_hbm, right_new_hbm, left_out_hbm, right_out_hbm,
-                 left_new, right_new, left_out, right_out, sems, *root_scratch):
-    dp, ow = lax.axis_index("dp"), lax.axis_index("owner")
-    writes = [pltpu.make_async_copy(src, dst, sems.at[i]) for i, (src, dst) in enumerate((
-        (left_new, left_new_hbm), (right_new, right_new_hbm), (left_out, left_out_hbm), (right_out, right_out_hbm)))]
     block = ow * SLOTS
     for r in range(SLOTS):
         block = jnp.where(owner_slot[r, ow] == dp, ow * SLOTS + r, block)
     hits = jnp.int32(0)
     for i in range(REFRESH):
         hits = hits + jnp.where(refresh[i] == block, jnp.int32(1), jnp.int32(0))
+    hit[0] = hits
+    for copy in stats:
+        copy.wait()
+    go.finish()
+
+
+vmem, smem, hbm = (pl.BlockSpec(memory_space=space) for space in (pltpu.VMEM, pltpu.SMEM, pltpu.HBM))
+
+
+def own(space, dtype, *lead):
+    return space(lead + (N, N), dtype)
+
+
+def reduce_scatter(*arrays):
+    vm = lambda *shape: pltpu.VMEM(shape + (N,), bf16)
+    return pl.pallas_call(
+        reduce_kernel,
+        out_shape=(pltpu.SMEM((1,), jnp.int32),) + tuple(own(pltpu.VMEM, dtype) for dtype in (bf16, f32, f32, bf16, bf16)),
+        in_specs=[smem] * 2 + [hbm] * 5,
+        out_specs=[smem] + [vmem] * 5,
+        scratch_shapes=[
+            vm(SLOTS, N), vm(SLOTS, N), vm(2, 2, RAH), vm(2, 2, RA), vm(RA), vm(XS, RB), vm(XS, RB), vm(2, RBH), vm(2, RB),
+            vm(2, 2, RAH), vm(2, RBH), vm(RA),
+            pltpu.SemaphoreType.DMA((23,)), pltpu.SemaphoreType.DMA((23,)), pltpu.SemaphoreType.DMA((SLOTS + 4,)),
+        ],
+        compiler_params=pltpu.CompilerParams(collective_id=0, has_side_effects=True, vmem_limit_bytes=56 * 2**20),
+        name="reduce_scatter",
+    )(*arrays)
+
+
+def local_kernel(hit, g, left_stat, right_stat, left_root, right_root,
+                 update, left_new_hbm, right_new_hbm, left_out_hbm, right_out_hbm,
+                 left_new, right_new, left_out, right_out, sems, *root_scratch):
+    writes = [pltpu.make_async_copy(src, dst, sems.at[i]) for i, (src, dst) in enumerate((
+        (left_new, left_new_hbm), (right_new, right_new_hbm), (left_out, left_out_hbm), (right_out, right_out_hbm)))]
     low = g[...]
     low_t = low.T
     weight = (1.0 - decay_rate) / N
@@ -262,11 +262,11 @@
     writes[0].start()
     writes[1].start()
 
-    @pl.when(hits > 0)
+    @pl.when(hit[0] > 0)
     def _():
         roots((left_new, right_new), (left_out, right_out), *root_scratch)
 
-    @pl.when(hits == 0)
+    @pl.when(hit[0] == 0)
     def _():
         left_out[...] = left_root[...]
         right_out[...] = right_root[...]
@@ -286,12 +286,12 @@
     return pl.pallas_call(
         local_kernel,
         out_shape=(own(pltpu.VMEM, bf16),) + tuple(own(pltpu.HBM, dtype) for dtype in mine[1:]),
-        in_specs=[smem] * 2 + [vmem] * 5,
+        in_specs=[smem] + [vmem] * 5,
         out_specs=[vmem] + [hbm] * 4,
         scratch_shapes=[own(pltpu.VMEM, dtype) for dtype in mine[1:]] + [pltpu.SemaphoreType.DMA((4,))]
         + [own(pltpu.VMEM, dtype, 2) for dtype in (bf16, bf16, bf16, bf16, f32, f32)]
         + [pltpu.VMEM((2, N, 3 * N), bf16), pltpu.VMEM((2, 3 * N, N), bf16)],
-        compiler_params=pltpu.CompilerParams(vmem_limit_bytes=32 * 2**20),
+        compiler_params=pltpu.CompilerParams(vmem_limit_bytes=48 * 2**20),
         name="local_step",
     )(*arrays)
 
@@ -403,9 +403,8 @@
 
 
 def body(grad_partials, owner_slot, refresh_blocks, left_stat, right_stat, left_root, right_root):
-    table = owner_slot.T
-    reduced = reduce_scatter(table, grad_partials[0], left_stat[0, 0], right_stat[0, 0], left_root[0, 0], right_root[0, 0])
-    update, *mine = local_step(table, refresh_blocks, *reduced)
+    reduced = reduce_scatter(owner_slot.T, refresh_blocks, grad_partials[0], left_stat[0, 0], right_stat[0, 0], left_root[0, 0], right_root[0, 0])
+    update, *mine = local_step(*reduced)
     gathered = write_out(all_gather(update))
     return (gathered[:, None], *(array[None, None] for array in mine))
 

time: 93.2 us -> 83.8 us (0.90)
  local copies, waits for them, and re-layouts: 8.73 us -> 0 us
    unnamed x16 -> x0, local copies, waits for them, and re-layouts: 8.73 us -> none
where the time goes in v4:
time: 83.8 us; the launch traced here: 83.7 us
  Pallas kernels  83 us (99%)
    pallas_call x1, Pallas kernels, all_gather(): pl.pallas_call(gather_kernel, out_shape=own(pltpu.VMEM, bf16, 16), in_spe...  44 us
    pallas_call x1, Pallas kernels, reduce_scatter(): pl.pallas_call(reduce_kernel, out_shape=(pltpu.SMEM((1,), jnp.int32),) +...  33.3 us
    pallas_call x1, Pallas kernels, write_out(): pl.pallas_call(write_kernel, out_shape=own(pltpu.HBM, bf16, 16), in_specs...  3.42 us
    pallas_call x1, Pallas kernels, local_step(): pl.pallas_call(local_kernel, out_shape=(own(pltpu.VMEM, bf16),) + tuple((...  2.26 us

profile of v4, /device:TPU:1, one launch (start us, length us, event | category | flops | bytes accessed | tf_op | source)
XLA Modules:
  0.0 83.7 jit_solution(10517308436890370825)
XLA Ops:
  0.6 33.3 %reduce_scatter.1 = (s32[1]{0:T(128)S(4)}, bf16[512,512]{1,0:T(8,128)(2,1)S(1)}, f32[512,512]{1,0:T(8,128)S(1)}, f32[512,512]{1,0:T(8,128)S(1)}, bf16[512,512]{1...) custom-call(s32[8,16]{1,0:T(8,128)} %bitcast.19, s32[32]{0:T(128)} %refresh.1, bf16[8,512,512]{2,1,0:T(8,128)(2,1)} %bitcast.14, ...), custom_call_target="tpu_custom_call" | custom-call | tf_op jit(solution)/shard_map/reduce_scatter/pallas_call | solution.py:237
  34.0 2.3 %local_step.1 = (bf16[512,512]{1,0:T(8,128)(2,1)S(1)}, f32[512,512]{1,0:T(8,128)}, f32[512,512]{1,0:T(8,128)}, bf16[512,512]{1,0:T(8,128)(2,1)}, bf16[512,512]{1,0:T(8,128)(2,1)}) custom-call(s32[1]{0:T(128)S(4)} %get-tuple-element.16.hit, bf16[512,512]{1,0:T(8,128)(2,1)S(1)} %get-tuple-element.17.g, f32[512,512]{1,0:T(8,128)S(1)} %get-tuple-element.18.left_stat, ...), custom_call_target="tpu_custom_call" | custom-call | tf_op jit(solution)/shard_map/local_step/pallas_call | solution.py:286
  36.3 44.0 %all_gather.1.src = bf16[16,512,512]{2,1,0:T(8,128)(2,1)S(1)} custom-call(bf16[512,512]{1,0:T(8,128)(2,1)S(1)} %get-tuple-element.22.update), custom_call_target="tpu_custom_call" | custom-call | tf_op jit(solution)/shard_map/all_gather/pallas_call | solution.py:374
  80.2 3.4 %write_out.1 = bf16[16,512,512]{2,1,0:T(8,128)(2,1)} custom-call(bf16[16,512,512]{2,1,0:T(8,128)(2,1)S(1)} %all_gather.1.src), custom_call_target="tpu_custom_call" | custom-call | tf_op jit(solution)/shard_map/write_out/pallas_call | solution.py:394

commit v5 on v2

--- a/solution.py
+++ b/solution.py
@@ -56,10 +56,10 @@
             copy.wait_send()
 
 
-RY, RYH = 288, 144
-RZ, RZH = N - RY, (N - RY) // 2
-Y_ALL, Y_LO, Y_HI = pl.ds(0, RY), pl.ds(0, RYH), pl.ds(RYH, RYH)
-Z_ALL, Z_LO, Z_HI = pl.ds(RY, RZ), pl.ds(RY, RZH), pl.ds(RY + RZH, RZH)
+RY, RYL = 288, 144
+RZ, RZL = N - RY, 112
+Y_ALL, Y_LO, Y_HI = pl.ds(0, RY), pl.ds(0, RYL), pl.ds(RYL, RY - RYL)
+Z_ALL, Z_LO, Z_HI = pl.ds(RY, RZ), pl.ds(RY, RZL), pl.ds(RY + RZL, RZ - RZL)
 
 
 def dot(a, b):
@@ -76,53 +76,75 @@
 
 
 def roots(stats, keep, kept, outs, d, q, u, hb, h, w, wide, tall):
-    rows = lax.broadcasted_iota(jnp.int32, (N, N), 0)
-    cols = lax.broadcasted_iota(jnp.int32, (N, N), 1)
-    both = range(2)
+    both, strip = range(2), 128
+    upper, lower, half = pl.ds(0, N // 2), pl.ds(N // 2, N // 2), N // 2
+    rows = lax.broadcasted_iota(jnp.int32, (strip, N), 0)
+    cols = lax.broadcasted_iota(jnp.int32, (strip, N), 1)
     final = []
+
+    def product(left, right):
+        return dot(left[0:half, :], right[...]), dot(left[half:N, :], right[:, half:N])
+
+    def mirror(ref, top, corner):
+        ref[upper, :], ref[lower, half:N], ref[lower, 0:half] = top, corner, top[:, half:N].T
+
     for m in both:
-        eye = jnp.where(rows == cols, 1.0, 0.0).astype(f32)
-        stat = stats[m][...]
-        scale = total(stat * eye) * (2.0 / N)
+        diagonal = jnp.zeros((strip, strip), f32)
+        for at in range(0, N, strip):
+            diagonal = diagonal + jnp.where(rows == cols, 1.0, 0.0)[:, 0:strip] * stats[m][at:at + strip, at:at + strip]
+        scale = total(diagonal) * (2.0 / N)
         final.append(lax.rsqrt(jnp.sqrt(scale)))
-        first = (eye - stat * (1.0 / scale)) * 0.25
-        high, rest = split(first)
-        d[m] = high
-        h[m] = eye + first
-        hb[m] = (eye + first).astype(bf16)
-        wide[m, :, 0:N], wide[m, :, N:2 * N], wide[m, :, 2 * N:3 * N] = high, high, rest
-        tall[m, 0:N, :], tall[m, N:2 * N, :], tall[m, 2 * N:3 * N, :] = high, rest, high
+        quarter = 0.25 / scale
+        for at in range(0, N, strip):
+            here = pl.ds(at, strip)
+            eye = jnp.where(rows + at == cols, 1.0, 0.0).astype(f32)
+            first = 0.25 * eye - stats[m][here, :] * quarter
+            high, rest = split(first)
+            d[m, here, :] = high
+            h[m, here, :] = eye + first
+            hb[m, here, :] = (eye + first).astype(bf16)
+            wide[m, here, 0:N], wide[m, here, N:2 * N], wide[m, here, 2 * N:3 * N] = high, high, rest
+            for k, value in enumerate((high, rest, high)):
+                tall[m, pl.ds(k * N + at, strip), :] = value
+
     for sweep in range(ITERS):
-        for m in both:
-            if sweep > 0:
-                new = h[m] + dot(hb[m], d[m])
-                if sweep == ITERS - 1:
-                    outs[m][...] = jnp.where(keep, kept[m][...], (new * final[m]).astype(bf16))
-                    continue
-                h[m] = new
-                hb[m] = new.astype(bf16)
-            square = dot(d[m], d[m]) if sweep > 0 else dot(wide[m], tall[m])
-            w[m] = square
-            q[m] = square.astype(bf16)
+        if sweep < ITERS - 1:
+            for m in both:
+                top, corner = product(d.at[m], d.at[m]) if sweep > 0 else product(wide.at[m], tall.at[m])
+                w[m, upper, :], w[m, lower, half:N] = top, corner
+                mirror(q.at[m], top.astype(bf16), corner.astype(bf16))
+        if sweep > 0:
+            for m in both:
+                top, corner = product(hb.at[m], d.at[m])
+                top, corner = h[m, upper, :] + top, h[m, lower, half:N] + corner
+                if sweep < ITERS - 1:
+                    h[m, upper, :], h[m, lower, half:N] = top, corner
+                    mirror(hb.at[m], top.astype(bf16), corner.astype(bf16))
+                else:
+                    top, corner = (top * final[m]).astype(bf16), (corner * final[m]).astype(bf16)
+                    mirror(outs[m], top, corner)
+                    outs[m][...] = jnp.where(keep, kept[m][...], outs[m][...])
         if sweep == ITERS - 1:
             break
         for m in both:
-            cube = dot(d[m], q[m])
-            square = w[m]
-            u[m] = (3.75 * square + cube).astype(bf16)
-            w[m] = 2.5 * square + 5.0 * cube
+            top, corner = product(d.at[m], q.at[m])
+            square, square_corner = w[m, upper, :], w[m, lower, half:N]
+            mirror(u.at[m], (3.75 * square + top).astype(bf16), (3.75 * square_corner + corner).astype(bf16))
+            w[m, upper, :], w[m, lower, half:N] = 2.5 * square + 5.0 * top, 2.5 * square_corner + 5.0 * corner
         for m in both:
-            d[m] = (w[m] + dot(q[m], u[m])).astype(bf16)
+            top, corner = product(q.at[m], u.at[m])
+            mirror(d.at[m], (w[m, upper, :] + top).astype(bf16), (w[m, lower, half:N] + corner).astype(bf16))
 
 
 def step_kernel(owner_slot, refresh, partials_hbm, left_stat_hbm, right_stat_hbm, left_root_hbm, right_root_hbm,
                 out, left_new, right_new, left_out, right_out,
-                partials, left_stat, right_stat, left_root, right_root, g, update,
+                partials_a, partials_b, left_stat, right_stat, left_root, right_root, g, update,
                 st, ra1, ra2, ra3, rb1, sb, rb2, rb3, acc_a, acc_b, sum_a, send_sem, recv_sem, load_sem, *root_scratch):
-    loads = [pltpu.make_async_copy(partials_hbm.at[i], partials.at[i], load_sem.at[i]) for i in range(SLOTS)]
+    loads_a = [pltpu.make_async_copy(partials_hbm.at[i, A_ALL], partials_a.at[i], load_sem.at[i]) for i in range(SLOTS)]
+    loads_b = [pltpu.make_async_copy(partials_hbm.at[i, B_ALL], partials_b.at[i], load_sem.at[SLOTS + 4 + i]) for i in range(SLOTS)]
     stats = [pltpu.make_async_copy(src, dst, load_sem.at[SLOTS + i]) for i, (src, dst) in enumerate((
         (left_stat_hbm, left_stat), (right_stat_hbm, right_stat), (left_root_hbm, left_root), (right_root_hbm, right_root)))]
-    for copy in loads:
+    for copy in loads_a + loads_b:
         copy.start()
     x, yl, yh, z, c = position()
     dp, ow = lax.axis_index("dp"), lax.axis_index("owner")
@@ -136,7 +158,7 @@
     zp, zm = (dp, owner(1, 0)), (dp, owner(3, 0))
     yp, co = (dp, owner(0, 1)), (dp, owner(0, 0, 1))
     greet((xp, xm, yo, zp, zm, yp, co))
-    for copy in loads:
+    for copy in loads_a:
         copy.wait()
     go = Copies(send_sem, recv_sem)
 
@@ -150,7 +172,7 @@
     where = {(dx, dy): block_of(dx, dy) for dx in range(XS) for dy in range(2)}
 
     def stage(dx, dy, rows):
-        st[dx * 2 + dy, rows, :] = partials[where[dx, dy], rows, :]
+        st[dx * 2 + dy, rows, :] = (partials_a if rows is A_ALL else partials_b)[where[dx, dy]]
 
     def own(dx, dy, rows):
         return st.at[dx * 2 + dy, rows]
@@ -183,6 +205,8 @@
         sb[dx] = (st[dx * 2, B_ALL, :].astype(f32) + rb1[dx].astype(f32)).astype(bf16)
 
     first_a(1)
+    for copy in loads_b:
+        copy.wait()
     for copy in stats:
         copy.start()
     first_b(2)
@@ -313,10 +337,10 @@
         in_specs=[smem] * 2 + [hbm] * 5,
         out_specs=[vmem] * 5,
         scratch_shapes=[
-            vm(SLOTS, N), pltpu.VMEM((N, N), f32), pltpu.VMEM((N, N), f32), vm(N), vm(N), vm(N), vm(N),
+            vm(SLOTS, RA), vm(SLOTS, RB), pltpu.VMEM((N, N), f32), pltpu.VMEM((N, N), f32), vm(N), vm(N), vm(N), vm(N),
             vm(SLOTS, N), vm(2, 2, RAH), vm(2, 2, RA), vm(RA), vm(XS, RB), vm(XS, RB), vm(2, RBH), vm(2, RB),
             vm(2, 2, RAH), vm(2, RBH), vm(RA),
-            pltpu.SemaphoreType.DMA((copies,)), pltpu.SemaphoreType.DMA((copies,)), pltpu.SemaphoreType.DMA((SLOTS + 4,)),
+            pltpu.SemaphoreType.DMA((copies,)), pltpu.SemaphoreType.DMA((copies,)), pltpu.SemaphoreType.DMA((2 * SLOTS + 4,)),
             *[pltpu.VMEM((2, N, N), dtype) for dtype in (bf16, bf16, bf16, bf16, f32, f32)],
             pltpu.VMEM((2, N, 3 * N), bf16), pltpu.VMEM((2, 3 * N, N), bf16),
         ],

time: 83.2 us -> 80.8 us (0.971)
  Pallas kernels: 82.4 us -> 80 us
    pallas_call x1, Pallas kernels: 78 us -> 75.6 us  [whole_step(): pl.pallas_call(step_kernel, out_shape=(like(bf16, 16), like(f32), like(f3...]
where the time goes in v5:
time: 80.8 us; the launch traced here: 80.6 us
  Pallas kernels  80 us (99%)
    pallas_call x1, Pallas kernels, whole_step(): pl.pallas_call(step_kernel, out_shape=(like(bf16, 16), like(f32), like(f3...  75.6 us
    pallas_call x1, Pallas kernels, write_out(): pl.pallas_call(write_kernel, out_shape=tuple((jax.ShapeDtypeStruct(a.shap...  4.4 us

profile of v5, /device:TPU:1, one launch (start us, length us, event | category | flops | bytes accessed | tf_op | source)
XLA Modules:
  0.0 80.6 jit_solution(1203160923858689654)
XLA Ops:
  0.6 75.6 %whole_step.1 = (bf16[16,512,512]{2,1,0:T(8,128)(2,1)S(1)}, f32[512,512]{1,0:T(8,128)S(1)}, f32[512,512]{1,0:T(8,128)S(1)}, bf16[512,512]{1,0:T(8,128)(2,1)S(1)}, bf16[512,512]{1,0:T(8,128)(2,1)S(1)}) custom-call(s32[8,16]{1,0:T(8,128)} %bitcast.18, s32[32]{0:T(128)} %refresh.1, bf16[8,512,512]{2,1,0:T(8,128)(2,1)} %bitcast.13, f32[512,512]{1,0:T(8,128)} %bitcast.14, ...), custom_call_target="tpu_custom_call" | custom-call | tf_op jit(solution)/shard_map/whole_step/pallas_call | solution.py:334
  76.2 4.4 %write_out.1 = (bf16[16,512,512]{2,1,0:T(8,128)(2,1)}, f32[512,512]{1,0:T(8,128)}, f32[512,512]{1,0:T(8,128)}, bf16[512,512]{1,0:T(8,128)(2,1)}, bf16[512,512]{1,0:T(8,128)(2,1)}) custom-call(bf16[16,512,512]{2,1,0:T(8,128)(2,1)S(1)} %get-tuple-element.15.refs_0_, f32[512,512]{1,0:T(8,128)S(1)} %get-tuple-element.16.refs_1_, ...), custom_call_target="tpu_custom_call" | custom-call | tf_op jit(solution)/shard_map/write_out/pallas_call | solution.py:367

commit v6 on v5

--- a/solution.py
+++ b/solution.py
@@ -32,7 +32,7 @@
     barrier = pltpu.get_barrier_semaphore()
     for target in targets:
         pl.semaphore_signal(barrier, inc=1, device_id=target, device_id_type=MESH)
-    pl.semaphore_wait(barrier, len(targets))
+    return lambda: pl.semaphore_wait(barrier, len(targets))
 
 
 class Copies:
@@ -112,7 +112,12 @@
             for m in both:
                 top, corner = product(d.at[m], d.at[m]) if sweep > 0 else product(wide.at[m], tall.at[m])
                 w[m, upper, :], w[m, lower, half:N] = top, corner
-                mirror(q.at[m], top.astype(bf16), corner.astype(bf16))
+                (top, top_rest), (corner, corner_rest) = split(top), split(corner)
+                mirror(q.at[m], top, corner)
+                if sweep == 0:
+                    mirror(tall.at[m, pl.ds(0, N)], top, corner)
+                    mirror(tall.at[m, pl.ds(N, N)], top_rest, corner_rest)
+                    mirror(tall.at[m, pl.ds(2 * N, N)], top, corner)
         if sweep > 0:
             for m in both:
                 top, corner = product(hb.at[m], d.at[m])
@@ -122,12 +127,12 @@
                     mirror(hb.at[m], top.astype(bf16), corner.astype(bf16))
                 else:
                     top, corner = (top * final[m]).astype(bf16), (corner * final[m]).astype(bf16)
-                    mirror(outs[m], top, corner)
-                    outs[m][...] = jnp.where(keep, kept[m][...], outs[m][...])
+                    mirror(outs[m], jnp.where(keep, kept[m][upper, :], top), jnp.where(keep, kept[m][lower, half:N], corner))
+                    outs[m][lower, 0:half] = jnp.where(keep, kept[m][lower, 0:half], outs[m][lower, 0:half])
         if sweep == ITERS - 1:
             break
         for m in both:
-            top, corner = product(d.at[m], q.at[m])
+            top, corner = product(d.at[m], q.at[m]) if sweep > 0 else product(wide.at[m], tall.at[m])
             square, square_corner = w[m, upper, :], w[m, lower, half:N]
             mirror(u.at[m], (3.75 * square + top).astype(bf16), (3.75 * square_corner + corner).astype(bf16))
             w[m, upper, :], w[m, lower, half:N] = 2.5 * square + 5.0 * top, 2.5 * square_corner + 5.0 * corner
@@ -140,24 +145,24 @@
                 out, left_new, right_new, left_out, right_out,
                 partials_a, partials_b, left_stat, right_stat, left_root, right_root, g, update,
                 st, ra1, ra2, ra3, rb1, sb, rb2, rb3, acc_a, acc_b, sum_a, send_sem, recv_sem, load_sem, *root_scratch):
+    x, yl, yh, z, c = position()
+    dp, ow = lax.axis_index("dp"), lax.axis_index("owner")
+
+    def owner(dz, dy, dc=0):
+        return (((yh + dy) % 2) * ZS + (z + dz) % ZS) * 2 + (c + dc) % 2
+
+    xp = (((x + 1) % XS) * 2 + yl, ow)
+    xm = (((x + XS - 1) % XS) * 2 + yl, ow)
+    yo = (x * 2 + 1 - yl, ow)
+    zp, zm = (dp, owner(1, 0)), (dp, owner(3, 0))
+    yp, co = (dp, owner(0, 1)), (dp, owner(0, 0, 1))
+    met = greet((xp, xm, yo, zp, zm, yp, co))
     loads_a = [pltpu.make_async_copy(partials_hbm.at[i, A_ALL], partials_a.at[i], load_sem.at[i]) for i in range(SLOTS)]
     loads_b = [pltpu.make_async_copy(partials_hbm.at[i, B_ALL], partials_b.at[i], load_sem.at[SLOTS + 4 + i]) for i in range(SLOTS)]
     stats = [pltpu.make_async_copy(src, dst, load_sem.at[SLOTS + i]) for i, (src, dst) in enumerate((
         (left_stat_hbm, left_stat), (right_stat_hbm, right_stat), (left_root_hbm, left_root), (right_root_hbm, right_root)))]
     for copy in loads_a + loads_b:
         copy.start()
-    x, yl, yh, z, c = position()
-    dp, ow = lax.axis_index("dp"), lax.axis_index("owner")
-
-    def owner(dz, dy, dc=0):
-        return (((yh + dy) % 2) * ZS + (z + dz) % ZS) * 2 + (c + dc) % 2
-
-    xp = (((x + 1) % XS) * 2 + yl, ow)
-    xm = (((x + XS - 1) % XS) * 2 + yl, ow)
-    yo = (x * 2 + 1 - yl, ow)
-    zp, zm = (dp, owner(1, 0)), (dp, owner(3, 0))
-    yp, co = (dp, owner(0, 1)), (dp, owner(0, 0, 1))
-    greet((xp, xm, yo, zp, zm, yp, co))
     for copy in loads_a:
         copy.wait()
     go = Copies(send_sem, recv_sem)
@@ -178,7 +183,6 @@
         return st.at[dx * 2 + dy, rows]
 
     def first_a(dy):
-        stage(2, dy, A_ALL)
         go.start(("a1p", dy), own(2, dy, A_LO), ra1.at[0, dy], xp)
         go.start(("a1m", dy), own(2, dy, A_HI), ra1.at[1, dy], xm)
 
@@ -204,7 +208,10 @@
         go.arrived(("b1", dx))
         sb[dx] = (st[dx * 2, B_ALL, :].astype(f32) + rb1[dx].astype(f32)).astype(bf16)
 
+    stage(2, 1, A_ALL)
+    met()
     first_a(1)
+    stage(2, 0, A_ALL)
     for copy in loads_b:
         copy.wait()
     for copy in stats:
@@ -280,7 +287,6 @@
     mine("zY+", Y_ALL, zp)
     mine("zY-", Y_ALL, zm)
     mine("yZ", Z_ALL, yp)
-    mine("core", pl.ds(0, N), co)
     out[owner(0, 0)] = update[...]
 
     go.arrived("zZ+")
@@ -291,6 +297,7 @@
     pass_on("zZ2-", 1, 0, Z_HI, zm)
     pass_on("yZ+", 1, 0, Z_ALL, yp)
     share(1, 0, Z_ALL, "Z")
+    mine("core", pl.ds(0, N), co)
     go.arrived("yY")
     pass_on("pY+", 0, 1, Y_ALL, zp)
     pass_on("pY-", 0, 1, Y_ALL, zm)

time: 80.8 us -> 81.6 us (level)
  Pallas kernels: 80 us -> 80.9 us
    pallas_call x1, Pallas kernels: 75.6 us -> 76.5 us  [whole_step(): pl.pallas_call(step_kernel, out_shape=(like(bf16, 16), like(f32), like(f3...]
where the time goes in v6:
time: 81.6 us; the launch traced here: 81.5 us
  Pallas kernels  80.9 us (99%)
    pallas_call x1, Pallas kernels, whole_step(): pl.pallas_call(step_kernel, out_shape=(like(bf16, 16), like(f32), like(f3...  76.5 us
    pallas_call x1, Pallas kernels, write_out(): pl.pallas_call(write_kernel, out_shape=tuple((jax.ShapeDtypeStruct(a.shap...  4.4 us

profile of v6, /device:TPU:1, one launch (start us, length us, event | category | flops | bytes accessed | tf_op | source)
XLA Modules:
  0.0 81.5 jit_solution(6582345305346018221)
XLA Ops:
  0.6 76.5 %whole_step.1 = (bf16[16,512,512]{2,1,0:T(8,128)(2,1)S(1)}, f32[512,512]{1,0:T(8,128)S(1)}, f32[512,512]{1,0:T(8,128)S(1)}, bf16[512,512]{1,0:T(8,128)(2,1)S(1)}, bf16[512,512]{1,0:T(8,128)(2,1)S(1)}) custom-call(s32[8,16]{1,0:T(8,128)} %bitcast.18, s32[32]{0:T(128)} %refresh.1, bf16[8,512,512]{2,1,0:T(8,128)(2,1)} %bitcast.13, f32[512,512]{1,0:T(8,128)} %bitcast.14, ...), custom_call_target="tpu_custom_call" | custom-call | tf_op jit(solution)/shard_map/whole_step/pallas_call | solution.py:341
  77.1 4.4 %write_out.1 = (bf16[16,512,512]{2,1,0:T(8,128)(2,1)}, f32[512,512]{1,0:T(8,128)}, f32[512,512]{1,0:T(8,128)}, bf16[512,512]{1,0:T(8,128)(2,1)}, bf16[512,512]{1,0:T(8,128)(2,1)}) custom-call(bf16[16,512,512]{2,1,0:T(8,128)(2,1)S(1)} %get-tuple-element.15.refs_0_, f32[512,512]{1,0:T(8,128)S(1)} %get-tuple-element.16.refs_1_, ...), custom_call_target="tpu_custom_call" | custom-call | tf_op jit(solution)/shard_map/write_out/pallas_call | solution.py:374

commit v7 on v6

--- a/solution.py
+++ b/solution.py
@@ -113,8 +113,9 @@
                 top, corner = product(d.at[m], d.at[m]) if sweep > 0 else product(wide.at[m], tall.at[m])
                 w[m, upper, :], w[m, lower, half:N] = top, corner
                 (top, top_rest), (corner, corner_rest) = split(top), split(corner)
-                mirror(q.at[m], top, corner)
-                if sweep == 0:
+                if sweep > 0:
+                    mirror(q.at[m], top, corner)
+                else:
                     mirror(tall.at[m, pl.ds(0, N)], top, corner)
                     mirror(tall.at[m, pl.ds(N, N)], top_rest, corner_rest)
                     mirror(tall.at[m, pl.ds(2 * N, N)], top, corner)
@@ -137,7 +138,7 @@
             mirror(u.at[m], (3.75 * square + top).astype(bf16), (3.75 * square_corner + corner).astype(bf16))
             w[m, upper, :], w[m, lower, half:N] = 2.5 * square + 5.0 * top, 2.5 * square_corner + 5.0 * corner
         for m in both:
-            top, corner = product(q.at[m], u.at[m])
+            top, corner = product(q.at[m] if sweep > 0 else tall.at[m, pl.ds(0, N)], u.at[m])
             mirror(d.at[m], (w[m, upper, :] + top).astype(bf16), (w[m, lower, half:N] + corner).astype(bf16))
 
 
@@ -269,7 +270,7 @@
     raw = dot(dot(left_out[...], low).astype(bf16), right_out[...])
     full = low.astype(f32)
     graft = jnp.sqrt(total(full * full) * (1.0 / (N * N))) / jnp.sqrt(total(raw * raw) * (1.0 / (N * N)) + graft_eps)
-    update[...] = (raw * graft).astype(bf16)
+    update[Y_ALL, :] = (raw[0:RY] * graft).astype(bf16)
 
     def pass_on(name, dz, dy, rows, target):
         piece = out.at[owner(dz, dy), rows]
@@ -282,6 +283,7 @@
         go.start(name, update.at[rows], out.at[owner(0, 0), rows], target)
 
     mine("yY", Y_ALL, yp)
+    update[Z_ALL, :] = (raw[RY:N] * graft).astype(bf16)
     mine("zZ+", Z_ALL, zp)
     mine("zZ-", Z_ALL, zm)
     mine("zY+", Y_ALL, zp)

time: 81.6 us -> 81.6 us (level)
  no operation moved by 1% of the time
where the time goes in v7:
time: 81.6 us; the launch traced here: 81.5 us
  Pallas kernels  80.9 us (99%)
    pallas_call x1, Pallas kernels, whole_step(): pl.pallas_call(step_kernel, out_shape=(like(bf16, 16), like(f32), like(f3...  76.5 us
    pallas_call x1, Pallas kernels, write_out(): pl.pallas_call(write_kernel, out_shape=tuple((jax.ShapeDtypeStruct(a.shap...  4.4 us

profile of v7, /device:TPU:1, one launch (start us, length us, event | category | flops | bytes accessed | tf_op | source)
XLA Modules:
  0.0 81.5 jit_solution(12480067290780279455)
XLA Ops:
  0.6 76.5 %whole_step.1 = (bf16[16,512,512]{2,1,0:T(8,128)(2,1)S(1)}, f32[512,512]{1,0:T(8,128)S(1)}, f32[512,512]{1,0:T(8,128)S(1)}, bf16[512,512]{1,0:T(8,128)(2,1)S(1)}, bf16[512,512]{1,0:T(8,128)(2,1)S(1)}) custom-call(s32[8,16]{1,0:T(8,128)} %bitcast.18, s32[32]{0:T(128)} %refresh.1, bf16[8,512,512]{2,1,0:T(8,128)(2,1)} %bitcast.13, f32[512,512]{1,0:T(8,128)} %bitcast.14, ...), custom_call_target="tpu_custom_call" | custom-call | tf_op jit(solution)/shard_map/whole_step/pallas_call | solution.py:343
  77.1 4.4 %write_out.1 = (bf16[16,512,512]{2,1,0:T(8,128)(2,1)}, f32[512,512]{1,0:T(8,128)}, f32[512,512]{1,0:T(8,128)}, bf16[512,512]{1,0:T(8,128)(2,1)}, bf16[512,512]{1,0:T(8,128)(2,1)}) custom-call(bf16[16,512,512]{2,1,0:T(8,128)(2,1)S(1)} %get-tuple-element.15.refs_0_, f32[512,512]{1,0:T(8,128)S(1)} %get-tuple-element.16.refs_1_, ...), custom_call_target="tpu_custom_call" | custom-call | tf_op jit(solution)/shard_map/write_out/pallas_call | solution.py:376
